TPU v7x, 32 devices: a whole 2x2x4 slice. The times are simulated.
32 devices in a mesh: tm: 8 (over z, x), cuts: 4 (over y, core).
Axes of the slice: x: 2, y: 2, z: 4, core: 2. Of those that a mesh axis runs over, the one named last changes fastest.
Arguments:
- start_image: float32 [32, 2, 128, 256], P(('cuts', 'tm')), parts along dimension 0, may hold values from -6 to 6
- sensitivity: bfloat16 [32, 2, 128, 256], P('cuts'), parts along dimension 0, may hold values from -2 to 2
- kspace: bfloat16 [32, 8, 2, 128, 256], P(('cuts', 'tm')), parts along dimension 0, may hold values from -6 to 6
- sampled: int32 [32, 8, 256], P(('cuts', 'tm')), parts along dimension 0, may hold values from 0 to 1
- offsets: int32 [8, 2], P('cuts'), parts along dimension 0, may hold values from 0 to 15
Outputs:
- reconstruction: float32 [32, 2, 128, 256], P(('cuts', 'tm')), parts along dimension 0
There are 4 independent parts, one for each index of `cuts`. A program takes and returns all parts, laid end to end along the dimension named above; each array names one. Nothing has to cross between parts.
All inputs are finite; a program needn't handle non-finite values. Where the computation divides by a largest or mean magnitude, that divisor is 1e-20 or more.
Results may differ from a plain program's by a relative error of at most 0.0037.
Values sent between devices are 32-bit elements; how exact they have to be, the bound alone decides.
No kernel may reach another device: no remote copies, remote signals or barrier semaphores. Data moves between devices by JAX's collectives and lax.ppermute only.
A program may use at most 64 MiB of HBM per device.

v0:
```python
import math

import jax
import jax.numpy as jnp
import ml_dtypes
import numpy as np
from jax import lax
from jax.experimental import pallas as pl
from jax.experimental.pallas import tpu as pltpu
from jax.sharding import PartitionSpec as P

BS = 16
ITERS = 2
NEWTON = 4
LANES = 128
SUBLANES = 8


shrink_ratio = 0.5
epsilon = 1e-06


def dft_tables(length):
    indices = jnp.arange(length, dtype=jnp.int32)
    phases = indices[:, None] * indices[None, :] % length
    angles = phases.astype(jnp.float32) * (2.0 * math.pi / length)
    norm_scale = 1.0 / math.sqrt(length)
    return (
        (jnp.cos(angles) * norm_scale).astype(jnp.bfloat16),
        (jnp.sin(angles) * norm_scale).astype(jnp.bfloat16),
    )


def forward(real_part, imag_part, cosine_table, sine_table):
    out_real = jnp.dot(real_part, cosine_table, preferred_element_type=jnp.float32) + jnp.dot(
        imag_part, sine_table, preferred_element_type=jnp.float32
    )
    out_imag = jnp.dot(imag_part, cosine_table, preferred_element_type=jnp.float32) - jnp.dot(
        real_part, sine_table, preferred_element_type=jnp.float32
    )
    return (out_real, out_imag)


def inverse(real_part, imag_part, cosine_table, sine_table):
    out_real = jnp.dot(real_part, cosine_table, preferred_element_type=jnp.float32) - jnp.dot(
        imag_part, sine_table, preferred_element_type=jnp.float32
    )
    out_imag = jnp.dot(imag_part, cosine_table, preferred_element_type=jnp.float32) + jnp.dot(
        real_part, sine_table, preferred_element_type=jnp.float32
    )
    return (out_real, out_imag)


def coil_spectra(field, sens_real, sens_imag, cosine_table, sine_table):
    coils, width, length = sens_real.shape
    coil_real = (
        (sens_real * field[0] - sens_imag * field[1])
        .astype(jnp.bfloat16)
        .reshape(coils * width, length)
    )
    coil_imag = (
        (sens_real * field[1] + sens_imag * field[0])
        .astype(jnp.bfloat16)
        .reshape(coils * width, length)
    )
    spec_real, spec_imag = forward(coil_real, coil_imag, cosine_table, sine_table)
    return (spec_real.reshape(coils, width, length), spec_imag.reshape(coils, width, length))


def frame_terms(field, sensitivity, data, lines, cosine_table, sine_table):
    sens_real = sensitivity[:, 0].astype(jnp.float32)
    sens_imag = sensitivity[:, 1].astype(jnp.float32)
    coils, width, length = sens_real.shape
    weight = lines.astype(jnp.float32)[:, None, :]
    spec_real, spec_imag = coil_spectra(field, sens_real, sens_imag, cosine_table, sine_table)
    misfit_real = (weight * (spec_real - data[:, 0].astype(jnp.float32))).astype(jnp.bfloat16)
    misfit_imag = (weight * (spec_imag - data[:, 1].astype(jnp.float32))).astype(jnp.bfloat16)
    back_real, back_imag = inverse(
        misfit_real.reshape(coils * width, length),
        misfit_imag.reshape(coils * width, length),
        cosine_table,
        sine_table,
    )
    back_real = back_real.reshape(coils, width, length)
    back_imag = back_imag.reshape(coils, width, length)
    grad_real = jnp.sum(sens_real * back_real + sens_imag * back_imag, axis=0)
    grad_imag = jnp.sum(sens_real * back_imag - sens_imag * back_real, axis=0)
    gradient = jnp.stack([grad_real, grad_imag])
    numerator = jnp.sum(gradient * gradient)
    probe_real, probe_imag = coil_spectra(gradient, sens_real, sens_imag, cosine_table, sine_table)
    denominator = jnp.sum(weight * (probe_real * probe_real + probe_imag * probe_imag))
    return (gradient, numerator, denominator)


def shrink(casorati):
    highest = lax.Precision.HIGHEST
    gram = jnp.einsum("bfv,bgv->bfg", casorati, casorati, precision=highest)
    frames = gram.shape[1]
    identity = jnp.eye(frames, dtype=jnp.float32)
    shrink_level = shrink_ratio * jnp.trace(gram, axis1=1, axis2=2) / frames + epsilon
    system = gram + shrink_level[:, None, None] * identity
    row_bound = jnp.max(jnp.sum(jnp.abs(system), axis=2), axis=1)
    approx = identity[None] / row_bound[:, None, None]
    for newton in range(NEWTON):
        product = jnp.einsum("bfg,bgh->bfh", system, approx, precision=highest)
        approx = jnp.einsum("bfg,bgh->bfh", approx, 2.0 * identity - product, precision=highest)
    return casorati - shrink_level[:, None, None] * jnp.einsum(
        "bfg,bgv->bfv", approx, casorati, precision=highest
    )


def to_blocks(field):
    frames, parts, width, length = field.shape
    blocks = field.reshape(frames, parts, width // BS, BS, length // BS, BS)
    blocks = blocks.transpose(2, 4, 0, 1, 3, 5)
    return blocks.reshape(width // BS * (length // BS), frames, parts * BS * BS)


def from_blocks(blocks, width, length):
    frames = blocks.shape[1]
    field = blocks.reshape(width // BS, length // BS, frames, 2, BS, BS)
    field = field.transpose(2, 3, 0, 4, 1, 5)
    return field.reshape(frames, 2, width, length)


def whole_body(start_image, sensitivity, kspace, sampled, offsets):
    width, length = (start_image.shape[2], start_image.shape[3])
    cosine_table, sine_table = dft_tables(length)
    estimate = start_image

    def per_frame(frame_items):
        field, data, lines = frame_items
        return frame_terms(field, sensitivity, data, lines, cosine_table, sine_table)

    for iteration in range(ITERS):
        gradient, numerator, denominator = lax.map(per_frame, (estimate, kspace, sampled))
        offset_pair = offsets[iteration]
        totals = lax.psum((jnp.sum(numerator), jnp.sum(denominator)), "tm")
        step_length = totals[0] / (totals[1] + epsilon)
        moved = estimate - step_length * gradient
        rolled = jnp.roll(moved, (offset_pair[0], offset_pair[1]), axis=(2, 3))
        casorati = lax.all_to_all(to_blocks(rolled), "tm", split_axis=0, concat_axis=1, tiled=True)
        shrunk = shrink(casorati)
        returned = lax.all_to_all(shrunk, "tm", split_axis=1, concat_axis=0, tiled=True)
        placed = from_blocks(returned, width, length)
        estimate = jnp.roll(placed, (-offset_pair[0], -offset_pair[1]), axis=(2, 3))
    return estimate


def block_of(column, shift, length):
    return lax.rem(column + shift, length) // BS


def iota(shape, dim):
    return lax.broadcasted_iota(jnp.int32, shape, dim)


def wide_tables(length):
    indices = np.arange(length, dtype=np.int32)
    phases = indices[:, None] * indices[None, :] % length
    angles = phases.astype(np.float32) * np.float32(2.0 * math.pi / length)
    norm_scale = np.float32(1.0 / math.sqrt(length))
    cosine = (np.cos(angles) * norm_scale).astype(ml_dtypes.bfloat16)
    sine = (np.sin(angles) * norm_scale).astype(ml_dtypes.bfloat16)
    ahead = np.block([[cosine, -sine], [sine, cosine]])
    back = np.block([[cosine, sine], [-sine, cosine]])
    return ahead, back


def pair_list(frames):
    return [(f, g) for f in range(frames) for g in range(f, frames)]


def pair_select(frames, lanes):
    table = np.zeros((frames * frames, lanes), np.float32)
    for place, (f, g) in enumerate(pair_list(frames)):
        table[f * frames + g, place] = 1.0
        table[g * frames + f, place] = 1.0
    return table


def exact_dot(a, b, dims=(((1,), (0,)), ((), ()))):
    return lax.dot_general(a, b, dims, precision=lax.Precision.HIGHEST, preferred_element_type=jnp.float32)


def mxu(a, b):
    return jnp.dot(a, b, preferred_element_type=jnp.float32)


def fold(x):
    rows, length = x.shape
    return jnp.sum(x.reshape(rows // 8, 8, length), axis=0)


def pack_kernel(offsets_ref, start_ref, lines_ref, out_ref):
    shift = offsets_ref[0, 0]
    strips = out_ref.shape[0]
    for part in range(2):
        rolled = pltpu.roll(start_ref[0, part], shift, 0)
        out_ref[:, part * BS : (part + 1) * BS, :] = rolled.reshape(strips, BS, rolled.shape[1])
    lines = lines_ref[0].astype(jnp.float32)
    coils = lines.shape[0]
    for strip in range(strips):
        out_ref[strip, 2 * BS : 2 * BS + coils, :] = lines


def frame_kernel(offsets_ref, start_ref, sens_ref, data_ref, lines_ref, ahead_ref, back_ref, out_ref, grad, num, den, left, right):
    step = pl.program_id(0)
    coils, _, rows, length = sens_ref.shape
    weight = lines_ref[0].astype(jnp.float32)

    @pl.when(step == 0)
    def _():
        num[...] = jnp.zeros_like(num)
        den[...] = jnp.zeros_like(den)

    def coil_image(a, b):
        for c in range(coils):
            sr = sens_ref[c, 0].astype(jnp.float32)
            si = sens_ref[c, 1].astype(jnp.float32)
            at = slice(c * rows, (c + 1) * rows)
            left[at, :length] = (sr * a - si * b).astype(jnp.bfloat16)
            left[at, length:] = (sr * b + si * a).astype(jnp.bfloat16)

    coil_image(start_ref[0, 0], start_ref[0, 1])
    spec = mxu(left[...], ahead_ref[...])
    for c in range(coils):
        at = slice(c * rows, (c + 1) * rows)
        w = weight[c : c + 1]
        right[at, :length] = (w * (spec[at, :length] - data_ref[0, c, 0].astype(jnp.float32))).astype(jnp.bfloat16)
        right[at, length:] = (w * (spec[at, length:] - data_ref[0, c, 1].astype(jnp.float32))).astype(jnp.bfloat16)
    home = mxu(right[...], back_ref[...])
    gr = jnp.zeros((rows, length), jnp.float32)
    gi = jnp.zeros((rows, length), jnp.float32)
    for c in range(coils):
        sr = sens_ref[c, 0].astype(jnp.float32)
        si = sens_ref[c, 1].astype(jnp.float32)
        at = slice(c * rows, (c + 1) * rows)
        br, bi = home[at, :length], home[at, length:]
        gr = gr + (sr * br + si * bi)
        gi = gi + (sr * bi - si * br)
    where = pl.ds(pl.multiple_of(step * rows, rows), rows)
    grad[0, where, :] = gr
    grad[1, where, :] = gi
    num[...] += fold(gr * gr + gi * gi)
    coil_image(gr, gi)
    probe = mxu(left[...], ahead_ref[...])
    total = jnp.zeros((8, length), jnp.float32)
    for c in range(coils):
        at = slice(c * rows, (c + 1) * rows)
        pr, pi = probe[at, :length], probe[at, length:]
        total = total + weight[c : c + 1] * fold(pr * pr + pi * pi)
    den[...] += total

    @pl.when(step == pl.num_programs(0) - 1)
    def _():
        shift = offsets_ref[0, 0]
        strips = out_ref.shape[0]
        for part in range(2):
            rolled = pltpu.roll(grad[part], shift, 0)
            out_ref[:, part * BS : (part + 1) * BS, :] = rolled.reshape(strips, BS, length)
        sums = jnp.where(
            iota((8, length), 0) == 0,
            jnp.sum(num[...], axis=0, keepdims=True),
            jnp.sum(den[...], axis=0, keepdims=True),
        )
        for strip in range(strips):
            out_ref[strip, 2 * BS : 2 * BS + 8, :] = sums


def strip_kernel(offsets_ref, sens_ref, out_ref, both, sems):
    axis = out_ref.shape
    coils, _, width, length = sens_ref.shape
    strips = width // BS
    me = lax.axis_index("tm")
    before = lax.rem(me + strips - 1, strips)
    first = pltpu.make_async_copy(
        sens_ref.at[:, :, pl.ds(pl.multiple_of(before * BS, BS), BS), :], both.at[0], sems.at[0]
    )
    second = pltpu.make_async_copy(
        sens_ref.at[:, :, pl.ds(pl.multiple_of(me * BS, BS), BS), :], both.at[1], sems.at[1]
    )
    first.start()
    second.start()
    first.wait()
    second.wait()
    shift = offsets_ref[0, 0]
    for c in range(coils):
        for part in range(2):
            rows = jnp.concatenate([both[0, c, part], both[1, c, part]], axis=0).astype(jnp.float32)
            out_ref[c, part] = pltpu.roll(rows, shift, 0)[BS:]


def newton_inverse(system, held, other, frames):
    lanes = system[0].shape[1]
    place = iota((frames, lanes), 0)
    unit = [(place == f).astype(jnp.float32) for f in range(frames)]
    sums = sum(jnp.abs(tile) for tile in system)
    bound = jnp.max(sums, axis=0, keepdims=True)
    for f in range(frames):
        held[f * frames : (f + 1) * frames, :] = system[f]
    approx = [unit[f] / bound for f in range(frames)]

    def times(ref, tiles):
        out = []
        for f in range(frames):
            terms = [ref[f * frames + g : f * frames + g + 1, :] * tiles[g] for g in range(frames)]
            while len(terms) > 1:
                terms = [a + b for a, b in zip(terms[::2], terms[1::2])]
            out.append(terms[0])
        return out

    for newton in range(NEWTON):
        for f in range(frames):
            other[f * frames : (f + 1) * frames, :] = approx[f]
        product = times(held, approx)
        approx = times(other, [2.0 * unit[f] - product[f] for f in range(frames)])
    return approx


def shrink_factors(gram, held, other, frames):
    lanes = gram.shape[1]
    place = iota((frames, lanes), 0)
    tiles = [gram[f * frames : (f + 1) * frames, :] for f in range(frames)]
    trace = sum(gram[f * frames + f : f * frames + f + 1, :] for f in range(frames))
    level = shrink_ratio * trace / frames + epsilon
    system = [tiles[f] + jnp.where(place == f, level, 0.0) for f in range(frames)]
    approx = newton_inverse(system, held, other, frames)
    return jnp.concatenate([level * tile for tile in approx], axis=0)


def middle_kernel(
    offsets_ref, image_ref, first_ref, sens_ref, ahead_ref, back_ref,
    out_ref, own_ref, est_ref, grad_ref,
    terms, held, other, spread, left, right,
):
    frames = image_ref.shape[0]
    coils, _, _, length = sens_ref.shape
    pairs = pair_list(frames)
    strip = 2 * BS
    numer = jnp.zeros((1, length), jnp.float32)
    denom = jnp.zeros((1, length), jnp.float32)
    for f in range(frames):
        numer = numer + first_ref[f, strip : strip + 1, :]
        denom = denom + first_ref[f, strip + 1 : strip + 2, :]
    numer = jnp.sum(numer, axis=1, keepdims=True)
    denom = jnp.sum(denom, axis=1, keepdims=True)
    step = numer / (denom + epsilon)
    for f in range(frames):
        est_ref[f] = image_ref[f, :strip, :] - step * first_ref[f, :strip, :]
    for f, g in pairs:
        tile = fold(est_ref[f] * est_ref[g])
        for place in {f * frames + g, g * frames + f}:
            for half in range(length // LANES):
                terms[half, place * 8 : place * 8 + 8, :] = tile[:, half * LANES : (half + 1) * LANES]
    count = frames * frames
    sums = jnp.concatenate(
        [sum(terms[half, pl.ds(s, count, stride=8), :] for s in range(8)) for half in range(length // LANES)], axis=1
    )
    shift = offsets_ref[0, 1]
    tall = (block_of(iota((length, LANES), 0), shift, length) == iota((length, LANES), 1)).astype(jnp.float32)
    broad = (block_of(iota((LANES, length), 1), shift, length) == iota((LANES, length), 0)).astype(jnp.float32)
    factors = shrink_factors(exact_dot(sums, tall), held, other, frames)
    spread[...] = exact_dot(factors, broad)
    moved = [est_ref[f] for f in range(frames)]
    for f in range(frames):
        total = spread[f * frames : f * frames + 1, :] * moved[0]
        for g in range(1, frames):
            total = total + spread[f * frames + g : f * frames + g + 1, :] * moved[g]
        grad_ref[f] = moved[f] - total
    for f in range(frames):
        est_ref[f] = grad_ref[f]

    num = jnp.zeros((8, length), jnp.float32)
    den = jnp.zeros((8, length), jnp.float32)
    group = left.shape[0] // (coils * BS)

    def coil_image(values):
        for k, (a, b) in enumerate(values):
            for c in range(coils):
                sr, si = sens_ref[c, 0], sens_ref[c, 1]
                at = slice((k * coils + c) * BS, (k * coils + c + 1) * BS)
                left[at, :length] = (sr * a - si * b).astype(jnp.bfloat16)
                left[at, length:] = (sr * b + si * a).astype(jnp.bfloat16)

    def passes(index, carry):
        num, den = carry
        at_frame = [index * group + k for k in range(group)]
        coil_image(
            [
                (
                    est_ref[f, :BS, :] - image_ref[f, :BS, :],
                    est_ref[f, BS:strip, :] - image_ref[f, BS:strip, :],
                )
                for f in at_frame
            ]
        )
        weights = [image_ref[f, strip : strip + coils, :] for f in at_frame]
        spec = mxu(left[...], ahead_ref[...])
        for k in range(group):
            for c in range(coils):
                at = slice((k * coils + c) * BS, (k * coils + c + 1) * BS)
                w = weights[k][c : c + 1]
                right[at, :length] = (w * spec[at, :length]).astype(jnp.bfloat16)
                right[at, length:] = (w * spec[at, length:]).astype(jnp.bfloat16)
        home = mxu(right[...], back_ref[...])
        values = []
        for k, f in enumerate(at_frame):
            gr = first_ref[f, :BS, :]
            gi = first_ref[f, BS:strip, :]
            for c in range(coils):
                at = slice((k * coils + c) * BS, (k * coils + c + 1) * BS)
                sr, si = sens_ref[c, 0], sens_ref[c, 1]
                br, bi = home[at, :length], home[at, length:]
                gr = gr + (sr * br + si * bi)
                gi = gi + (sr * bi - si * br)
            grad_ref[f, :BS, :] = gr
            grad_ref[f, BS:strip, :] = gi
            num = num + fold(gr * gr + gi * gi)
            values.append((gr, gi))
        coil_image(values)
        probe = mxu(left[...], ahead_ref[...])
        for k in range(group):
            for c in range(coils):
                at = slice((k * coils + c) * BS, (k * coils + c + 1) * BS)
                pr, pi = probe[at, :length], probe[at, length:]
                den = den + weights[k][c : c + 1] * fold(pr * pr + pi * pi)
        return num, den

    num, den = lax.fori_loop(0, frames // group, passes, (num, den))
    numer = jnp.sum(jnp.sum(num, axis=0, keepdims=True), axis=1, keepdims=True)
    denom = jnp.sum(jnp.sum(den, axis=0, keepdims=True), axis=1, keepdims=True)

    edge = lax.rem(offsets_ref[0, 0] - offsets_ref[1, 0] + BS, BS)
    low = [(iota((8, length), 0) + 8 * t >= edge) for t in range(BS // 8)]
    block = len(pairs)
    span = out_ref.shape[2]

    def rows_of(product):
        return [
            sum(product[p * BS + 8 * t : p * BS + 8 * t + 8] for p in range(2)) for t in range(BS // 8)
        ]

    def put(part, place, tile):
        for half in range(length // LANES):
            terms[half, (part * span + place) * 8 : (part * span + place) * 8 + 8, :] = tile[
                :, half * LANES : (half + 1) * LANES
            ]

    for part in range(2):
        for place in range(3 * block, span):
            put(part, place, jnp.zeros((8, length), jnp.float32))
    for place, (f, g) in enumerate(pairs):
        ef, eg, gf, gg = est_ref[f], est_ref[g], grad_ref[f], grad_ref[g]
        for kind, product in enumerate((ef * eg, ef * gg + eg * gf, gf * gg)):
            rows = rows_of(product)
            put(0, kind * block + place, sum(jnp.where(low[t], rows[t], 0.0) for t in range(BS // 8)))
            put(1, kind * block + place, sum(jnp.where(low[t], 0.0, rows[t]) for t in range(BS // 8)))
    shift = offsets_ref[1, 1]
    blocks = length // BS
    member = (block_of(iota((blocks, length), 1), shift, length) == iota((blocks, length), 0)).astype(jnp.float32)
    lane = iota((blocks, span), 1)
    packs = []
    for part in range(2):
        sums = jnp.concatenate(
            [
                sum(terms[half, pl.ds(part * span * 8 + s, span, stride=8), :] for s in range(8))
                for half in range(length // LANES)
            ],
            axis=1,
        )
        pack = exact_dot(member, sums, (((1,), (1,)), ((), ())))
        pack = jnp.where(lane == 3 * block, numer, jnp.where(lane == 3 * block + 1, denom, pack))
        own_ref[part * blocks : (part + 1) * blocks, :] = pack
        packs.append(pack)
    me = lax.axis_index("tm")
    strips = out_ref.shape[0]
    before = lax.rem(me + strips - 1, strips)
    for target in range(strips):
        out_ref[target] = jnp.where(before == target, packs[1], packs[0])


def last_kernel(offsets_ref, own_ref, heard_ref, est_ref, grad_ref, select_ref, out_ref, held, other, spread_low, spread_up):
    frames, strip, length = est_ref.shape
    strips, blocks, span = heard_ref.shape
    block = len(pair_list(frames))
    me = lax.axis_index("tm")
    numer = jnp.zeros((1, 1), jnp.float32)
    denom = jnp.zeros((1, 1), jnp.float32)
    for k in range(strips):
        numer = numer + heard_ref[k, 0:1, 3 * block : 3 * block + 1]
        denom = denom + heard_ref[k, 0:1, 3 * block + 1 : 3 * block + 2]
    step = numer / (denom + epsilon)
    after = lax.rem(me + 1, strips)
    before = lax.rem(me + strips - 1, strips)
    total = own_ref[...] + jnp.concatenate([heard_ref[after], heard_ref[before]], axis=0)
    cross = pltpu.roll(total, span - block, 1)
    square = pltpu.roll(total, span - 2 * block, 1)
    gram = total - step * cross + step * step * square
    gram = jnp.concatenate([gram, jnp.zeros((LANES - 2 * blocks, span), jnp.float32)], axis=0)
    gram = jnp.where(iota(gram.shape, 1) < block, gram, 0.0)
    gram = exact_dot(select_ref[...], gram, (((1,), (1,)), ((), ())))
    factors = shrink_factors(gram, held, other, frames)
    shift = offsets_ref[1, 1]
    column = block_of(iota((LANES, length), 1), shift, length)
    row = iota((LANES, length), 0)
    spread_low[...] = exact_dot(factors, (column == row).astype(jnp.float32))
    spread_up[...] = exact_dot(factors, (column + blocks == row).astype(jnp.float32))
    edge = lax.rem(offsets_ref[0, 0] - offsets_ref[1, 0] + BS, BS)
    moved = [est_ref[f] - step * grad_ref[f] for f in range(frames)]
    for t in range(BS // 8):
        low = iota((8, length), 0) + 8 * t >= edge
        for f in range(frames):
            total = [jnp.zeros((8, length), jnp.float32)] * 2
            for g in range(frames):
                at = f * frames + g
                factor = jnp.where(low, spread_low[at : at + 1, :], spread_up[at : at + 1, :])
                total = [total[p] + factor * moved[g][p * BS + 8 * t : p * BS + 8 * t + 8] for p in range(2)]
            for p in range(2):
                rows = slice(p * BS + 8 * t, p * BS + 8 * t + 8)
                out_ref[f, rows, :] = moved[f][rows] - total[p]


def place_kernel(offsets_ref, strips_ref, out_ref):
    strips, strip, length = strips_ref.shape
    width = strips * BS
    shift = lax.rem(width - offsets_ref[0, 0], width)
    for part in range(2):
        whole = strips_ref[:, part * BS : (part + 1) * BS, :].reshape(width, length)
        out_ref[0, part] = pltpu.roll(whole, shift, 0)


def vmem():
    return pl.BlockSpec(memory_space=pltpu.VMEM)


def smem():
    return pl.BlockSpec(memory_space=pltpu.SMEM)


def f32(*shape):
    return jax.ShapeDtypeStruct(shape, jnp.float32)


def exchange(blocks):
    return lax.all_to_all(blocks, "tm", split_axis=0, concat_axis=0, tiled=True)


def params():
    return pltpu.CompilerParams(vmem_limit_bytes=32 * 1024 * 1024)


def strips_body(start_image, sensitivity, kspace, sampled, offsets):
    _, _, width, length = start_image.shape
    coils = sensitivity.shape[0]
    strips = width // BS
    frames = strips
    ahead, back = (jnp.asarray(table) for table in wide_tables(length))
    strip = 2 * BS
    span = LANES
    blocks = length // BS

    packed = pl.pallas_call(
        pack_kernel,
        out_shape=f32(strips, strip + coils, length),
        in_specs=[smem(), vmem(), vmem()],
        out_specs=vmem(),
        compiler_params=params(),
        cost_estimate=pl.CostEstimate(flops=10**6, bytes_accessed=10**6, transcendentals=0),
    )(offsets, start_image, sampled)
    image = exchange(packed)

    rows = 2 * BS
    first = pl.pallas_call(
        frame_kernel,
        grid=(width // rows,),
        out_shape=f32(strips, strip + 8, length),
        in_specs=[
            smem(),
            pl.BlockSpec((1, 2, rows, length), lambda i: (0, 0, i, 0)),
            pl.BlockSpec((coils, 2, rows, length), lambda i: (0, 0, i, 0)),
            pl.BlockSpec((1, coils, 2, rows, length), lambda i: (0, 0, 0, i, 0)),
            pl.BlockSpec((1, coils, length), lambda i: (0, 0, 0)),
            vmem(),
            vmem(),
        ],
        out_specs=pl.BlockSpec((strips, strip + 8, length), lambda i: (0, 0, 0)),
        scratch_shapes=[
            pltpu.VMEM((2, width, length), jnp.float32),
            pltpu.VMEM((8, length), jnp.float32),
            pltpu.VMEM((8, length), jnp.float32),
            pltpu.VMEM((coils * rows, 2 * length), jnp.bfloat16),
            pltpu.VMEM((coils * rows, 2 * length), jnp.bfloat16),
        ],
        compiler_params=params(),
        cost_estimate=pl.CostEstimate(flops=24 * coils * width * length * length, bytes_accessed=4 * 10**6, transcendentals=0),
    )(offsets, start_image, sensitivity, kspace, sampled, ahead, back)
    first = exchange(first)

    sens = pl.pallas_call(
        strip_kernel,
        out_shape=f32(coils, 2, BS, length),
        in_specs=[smem(), pl.BlockSpec(memory_space=pl.ANY)],
        out_specs=vmem(),
        scratch_shapes=[pltpu.VMEM((2, coils, 2, BS, length), jnp.bfloat16), pltpu.SemaphoreType.DMA((2,))],
        compiler_params=params(),
        cost_estimate=pl.CostEstimate(flops=10**6, bytes_accessed=10**6, transcendentals=0),
    )(offsets, sensitivity)

    count = frames * frames
    group = 2
    sent, own, estimate, gradient = pl.pallas_call(
        middle_kernel,
        out_shape=(
            f32(strips, blocks, span),
            f32(2 * blocks, span),
            f32(frames, strip, length),
            f32(frames, strip, length),
        ),
        in_specs=[smem()] + [vmem()] * 5,
        out_specs=(vmem(),) * 4,
        scratch_shapes=[
            pltpu.VMEM((length // LANES, 2 * span * 8, LANES), jnp.float32),
            pltpu.VMEM((count, LANES), jnp.float32),
            pltpu.VMEM((count, LANES), jnp.float32),
            pltpu.VMEM((count, length), jnp.float32),
            pltpu.VMEM((group * coils * BS, 2 * length), jnp.bfloat16),
            pltpu.VMEM((group * coils * BS, 2 * length), jnp.bfloat16),
        ],
        compiler_params=params(),
        cost_estimate=pl.CostEstimate(flops=24 * coils * width * length * length, bytes_accessed=4 * 10**6, transcendentals=0),
    )(offsets, image, first, sens, ahead, back)
    heard = exchange(sent)

    returned = pl.pallas_call(
        last_kernel,
        out_shape=f32(frames, strip, length),
        in_specs=[smem()] + [vmem()] * 5,
        out_specs=vmem(),
        scratch_shapes=[
            pltpu.VMEM((count, LANES), jnp.float32),
            pltpu.VMEM((count, LANES), jnp.float32),
            pltpu.VMEM((count, length), jnp.float32),
            pltpu.VMEM((count, length), jnp.float32),
        ],
        compiler_params=params(),
    )(offsets, own, heard, estimate, gradient, jnp.asarray(pair_select(frames, span)))
    returned = exchange(returned)

    return pl.pallas_call(
        place_kernel,
        out_shape=f32(1, 2, width, length),
        in_specs=[smem(), vmem()],
        out_specs=vmem(),
        compiler_params=params(),
    )(offsets, returned)


def fits_strips(start_image, sensitivity, kspace, sampled, offsets):
    strips = lax.axis_size("tm")
    frames, _, width, length = start_image.shape
    coils = sensitivity.shape[0]
    kinds = 3 * len(pair_list(strips))
    return (
        frames == 1
        and width == strips * BS
        and strips == SUBLANES
        and coils % SUBLANES == 0
        and ITERS == 2
        and length % LANES == 0
        and 2 * (length // BS) <= LANES
        and kinds + 2 <= LANES
    )


def body(*args):
    return (strips_body if fits_strips(*args) else whole_body)(*args)


def solution(mesh):
    placed = (
        P(("cuts", "tm"), None, None, None),
        P("cuts", None, None, None),
        P(("cuts", "tm"), None, None, None, None),
        P(("cuts", "tm"), None, None),
        P("cuts", None),
    )
    return jax.shard_map(
        body,
        mesh=mesh,
        in_specs=placed,
        out_specs=P(("cuts", "tm"), None, None, None),
        check_vma=False,
    )
```

profile of v0, /device:TPU:0, one launch (start us, length us, event | category | flops | bytes accessed | tf_op | source)
XLA Modules:
  0.0 72.9 jit_solution(1619608045383894356)
XLA Ops:
  0.0 0.0 copy-start
  0.0 1.2 %copy-done = bf16[8,2,128,256]{3,2,1,0:T(8,128)(2,1)S(1)} copy-done((bf16[8,2,128,256]{3,2,1,0:T(8,128)(2,1)S(1)}, bf16[8,2,128,256]{3,2,1,0:T(8,128)(2,1)}, u32[]{:S(2)}) %copy-start) | copy-done | bytes 1048600
  1.2 0.0 copy-start.2
  1.2 0.9 %copy-done.2 = f32[1,2,128,256]{3,2,1,0:T(8,128)S(1)} copy-done((f32[1,2,128,256]{3,2,1,0:T(8,128)S(1)}, f32[1,2,128,256]{3,2,1,0:T(8,128)}, u32[]{:S(2)}) %copy-start.2) | copy-done | bytes 262168
  2.2 0.0 copy-start.5
  2.2 0.7 copy-done.5
  2.9 0.0 copy-start.7
  2.9 0.7 copy-done.7
  3.6 0.0 copy-start.9
  3.6 1.2 %copy-done.9 = bf16[1,8,2,128,256]{4,3,2,1,0:T(8,128)(2,1)S(1)} copy-done((bf16[1,8,2,128,256]{4,3,2,1,0:T(8,128)(2,1)S(1)}, bf16[1,8,2,128,256]{4,3,2,1,0:T(8,128)(2,1)}, u32[]{:S(2)}) %copy-start.9) | copy-done | bytes 1048600
  4.8 0.0 copy-start.10
  4.8 1.0 %copy-done.10 = bf16[512,512]{1,0:T(8,128)(2,1)S(1)} copy-done((bf16[512,512]{1,0:T(8,128)(2,1)S(1)}, bf16[512,512]{1,0:T(8,128)(2,1)}, u32[]{:S(2)}) %copy-start.10) | copy-done | bytes 524312
  5.8 0.0 copy-start.12
  5.8 1.0 %copy-done.12 = bf16[512,512]{1,0:T(8,128)(2,1)S(1)} copy-done((bf16[512,512]{1,0:T(8,128)(2,1)S(1)}, bf16[512,512]{1,0:T(8,128)(2,1)}, u32[]{:S(2)}) %copy-start.12) | copy-done | bytes 524312
  6.9 0.0 copy-start.3
  6.9 0.0 copy-start.6
  6.9 0.0 copy-start.8
  6.9 5.0 %shard_map.83 = f32[8,40,256]{2,1,0:T(8,128)} custom-call(s32[2,2]{1,0:T(2,128)S(1)} %copy-done.5, f32[1,2,128,256]{3,2,1,0:T(8,128)S(1)} %copy-done.2, bf16[8,2,128,256]{3,2,1,0:T(8,128)(2,1)S(1)} %copy-done, bf16[1,8,2,128,256]{4,3,2,1,0:T(8,128)(2,1)S(1)} %copy-done.9, s32[1,8,256]{2,1,0:T(8,128)S(1)} %copy-done.7, bf16[512,512]{1,0:T(8,128)(2,1)S(1)} %copy-done.12, ...), custom_call_target="tpu_custom_call" | custom-call | flops 1610612736 | bytes 4000000 | tf_op jit(solution)/shard_map/pallas_call | solution.py:574
  11.8 0.0 copy-start.1
  11.8 7.4 %all-to-all-start.1 = ((f32[8,40,256]{2,1,0:T(8,128)}), f32[8,40,256]{2,1,0:T(8,128)S(1)}, u32[]{:S(2)}, u32[]{:S(2)}) async-start(f32[8,40,256]{2,1,0:T(8,128)} %shard_map.83), calls=%async_computation.1 | async-start | bytes 655360 | tf_op jit(solution)/shard_map/all_to_all | solution.py:546
  19.3 0.0 copy-done.3
  19.3 0.0 copy-done.6
  19.3 0.0 copy-done.8
  19.3 1.3 %shard_map.82 = f32[8,40,256]{2,1,0:T(8,128)} custom-call(s32[2,2]{1,0:T(2,128)S(1)} %copy-done.6, f32[1,2,128,256]{3,2,1,0:T(8,128)S(1)} %copy-done.3, s32[1,8,256]{2,1,0:T(8,128)S(1)} %copy-done.8), custom_call_target="tpu_custom_call" | custom-call | flops 1000000 | bytes 1000000 | tf_op jit(solution)/shard_map/pallas_call | solution.py:563
  20.7 8.9 %all-to-all-done.1.first_ref = f32[8,40,256]{2,1,0:T(8,128)S(1)} async-done(((f32[8,40,256]{2,1,0:T(8,128)}), f32[8,40,256]{2,1,0:T(8,128)S(1)}, u32[]{:S(2)}, u32[]{:S(2)}) %all-to-all-start.1) | async-done | bytes 327712 | tf_op jit(solution)/shard_map/all_to_all | solution.py:546
  29.6 3.6 %all-to-all-start = ((f32[8,40,256]{2,1,0:T(8,128)}), f32[8,40,256]{2,1,0:T(8,128)S(1)}, u32[]{:S(2)}, u32[]{:S(2)}) async-start(f32[8,40,256]{2,1,0:T(8,128)} %shard_map.82), calls=%async_computation | async-start | bytes 655360 | tf_op jit(solution)/shard_map/all_to_all | solution.py:546
  33.2 0.0 copy-done.1
  33.2 0.0 copy-start.11
  33.2 0.0 copy-start.13
  33.2 0.7 shard_map.84.sens_ref
  33.9 9.1 %all-to-all-done.image_ref = f32[8,40,256]{2,1,0:T(8,128)S(1)} async-done(((f32[8,40,256]{2,1,0:T(8,128)}), f32[8,40,256]{2,1,0:T(8,128)S(1)}, u32[]{:S(2)}, u32[]{:S(2)}) %all-to-all-start) | async-done | bytes 327712 | tf_op jit(solution)/shard_map/all_to_all | solution.py:546
  43.0 0.0 copy-done.11
  43.0 0.0 copy-done.13
  43.0 5.9 %shard_map.85 = (f32[8,16,128]{2,1,0:T(8,128)S(1)}, f32[32,128]{1,0:T(8,128)S(1)}, f32[8,32,256]{2,1,0:T(8,128)S(1)}, f32[8,32,256]{2,1,0:T(8,128)S(1)}) custom-call(s32[2,2]{1,0:T(2,128)S(1)} %copy-done.6, f32[8,40,256]{2,1,0:T(8,128)S(1)} %all-to-all-done.image_ref, f32[8,40,256]{2,1,0:T(8,128)S(1)} %all-to-all-done.1.first_ref, ...), custom_call_target="tpu_custom_call" | custom-call | flops 1610612736 | bytes 4000000 | tf_op jit(solution)/shard_map/pallas_call | solution.py:612
  48.9 0.0 copy-start.4
  48.9 10.5 %all_to_all.20.heard_ref = f32[8,16,128]{2,1,0:T(8,128)S(1)} all-to-all(f32[8,16,128]{2,1,0:T(8,128)S(1)} %get-tuple-element.10), channel_id=1, replica_groups=mesh['tm'=8,'cuts'=4] {'tm'}, dimensions={0} | all-to-all | bytes 131072 | tf_op jit(solution)/shard_map/all_to_all | solution.py:546
  59.4 0.0 copy-done.4
  59.4 1.6 %shard_map.86 = f32[8,32,256]{2,1,0:T(8,128)S(1)} custom-call(s32[2,2]{1,0:T(2,128)S(1)} %copy-done.6, f32[32,128]{1,0:T(8,128)S(1)} %get-tuple-element.9.own_ref, f32[8,16,128]{2,1,0:T(8,128)S(1)} %all_to_all.20.heard_ref, f32[8,32,256]{2,1,0:T(8,128)S(1)} %get-tuple-element.11.est_ref, f32[8,32,256]{2,1,0:T(8,128)S(1)} %get-tuple-element.12.grad_ref, ...), custom_call_target="tpu_custom_call" | custom-call | tf_op jit(solution)/shard_map/pallas_call | solution.py:635
  61.0 10.6 %all_to_all.21.strips_ref = f32[8,32,256]{2,1,0:T(8,128)S(1)} all-to-all(f32[8,32,256]{2,1,0:T(8,128)S(1)} %shard_map.86), channel_id=1, replica_groups=mesh['tm'=8,'cuts'=4] {'tm'}, dimensions={0} | all-to-all | bytes 524288 | tf_op jit(solution)/shard_map/all_to_all | solution.py:546
  71.6 1.3 %shard_map.87 = f32[1,2,128,256]{3,2,1,0:T(8,128)} custom-call(s32[2,2]{1,0:T(2,128)S(1)} %copy-done.6, f32[8,32,256]{2,1,0:T(8,128)S(1)} %all_to_all.21.strips_ref), custom_call_target="tpu_custom_call" | custom-call | tf_op jit(solution)/shard_map/pallas_call | solution.py:650
Async XLA Ops:
  0.0 1.2 %copy-start = (bf16[8,2,128,256]{3,2,1,0:T(8,128)(2,1)S(1)}, bf16[8,2,128,256]{3,2,1,0:T(8,128)(2,1)}, u32[]{:S(2)}) copy-start(bf16[8,2,128,256]{3,2,1,0:T(8,128)(2,1)} %sens_ref.3) | copy-start | bytes 3145732
  1.2 0.9 %copy-start.2 = (f32[1,2,128,256]{3,2,1,0:T(8,128)S(1)}, f32[1,2,128,256]{3,2,1,0:T(8,128)}, u32[]{:S(2)}) copy-start(f32[1,2,128,256]{3,2,1,0:T(8,128)} %start_ref.3) | copy-start | bytes 786436
  2.2 0.7 copy-start.5
  2.9 0.7 copy-start.7
  3.6 1.2 %copy-start.9 = (bf16[1,8,2,128,256]{4,3,2,1,0:T(8,128)(2,1)S(1)}, bf16[1,8,2,128,256]{4,3,2,1,0:T(8,128)(2,1)}, u32[]{:S(2)}) copy-start(bf16[1,8,2,128,256]{4,3,2,1,0:T(8,128)(2,1)} %data_ref.1) | copy-start | bytes 3145732
  4.8 1.0 %copy-start.10 = (bf16[512,512]{1,0:T(8,128)(2,1)S(1)}, bf16[512,512]{1,0:T(8,128)(2,1)}, u32[]{:S(2)}) copy-start(bf16[512,512]{1,0:T(8,128)(2,1)} %constant.7.clone.back_ref) | copy-start | bytes 1572868
  5.8 1.0 %copy-start.12 = (bf16[512,512]{1,0:T(8,128)(2,1)S(1)}, bf16[512,512]{1,0:T(8,128)(2,1)}, u32[]{:S(2)}) copy-start(bf16[512,512]{1,0:T(8,128)(2,1)} %constant.6.clone.ahead_ref) | copy-start | bytes 1572868
  6.9 12.4 %copy-start.3 = (f32[1,2,128,256]{3,2,1,0:T(8,128)S(1)}, f32[1,2,128,256]{3,2,1,0:T(8,128)}, u32[]{:S(2)}) copy-start(f32[1,2,128,256]{3,2,1,0:T(8,128)} %start_ref.3) | copy-start | bytes 786436
  6.9 12.4 %copy-start.6 = (s32[2,2]{1,0:T(2,128)S(1)}, s32[2,2]{1,0:T(2,128)}, u32[]{:S(2)}) copy-start(s32[2,2]{1,0:T(2,128)} %offsets_ref.11) | copy-start | bytes 52
  6.9 12.4 %copy-start.8 = (s32[1,8,256]{2,1,0:T(8,128)S(1)}, s32[1,8,256]{2,1,0:T(8,128)}, u32[]{:S(2)}) copy-start(s32[1,8,256]{2,1,0:T(8,128)} %lines_ref.3) | copy-start | bytes 24580
  11.8 21.3 %copy-start.1 = (bf16[8,2,128,256]{3,2,1,0:T(8,128)(2,1)S(1)}, bf16[8,2,128,256]{3,2,1,0:T(8,128)(2,1)}, u32[]{:S(2)}) copy-start(bf16[8,2,128,256]{3,2,1,0:T(8,128)(2,1)} %sens_ref.3) | copy-start | bytes 3145732
  11.8 17.7 %all-to-all-start.1 = ((f32[8,40,256]{2,1,0:T(8,128)}), f32[8,40,256]{2,1,0:T(8,128)S(1)}, u32[]{:S(2)}, u32[]{:S(2)}) async-start(f32[8,40,256]{2,1,0:T(8,128)} %shard_map.83), calls=%async_computation.1 | async-start | bytes 655360 | tf_op jit(solution)/shard_map/all_to_all | solution.py:546
  29.6 13.4 %all-to-all-start = ((f32[8,40,256]{2,1,0:T(8,128)}), f32[8,40,256]{2,1,0:T(8,128)S(1)}, u32[]{:S(2)}, u32[]{:S(2)}) async-start(f32[8,40,256]{2,1,0:T(8,128)} %shard_map.82), calls=%async_computation | async-start | bytes 655360 | tf_op jit(solution)/shard_map/all_to_all | solution.py:546
  33.2 9.8 %copy-start.11 = (bf16[512,512]{1,0:T(8,128)(2,1)S(1)}, bf16[512,512]{1,0:T(8,128)(2,1)}, u32[]{:S(2)}) copy-start(bf16[512,512]{1,0:T(8,128)(2,1)} %constant.7.clone.back_ref) | copy-start | bytes 1572868
  33.2 9.8 %copy-start.13 = (bf16[512,512]{1,0:T(8,128)(2,1)S(1)}, bf16[512,512]{1,0:T(8,128)(2,1)}, u32[]{:S(2)}) copy-start(bf16[512,512]{1,0:T(8,128)(2,1)} %constant.6.clone.ahead_ref) | copy-start | bytes 1572868
  48.9 10.5 %copy-start.4 = (f32[64,128]{1,0:T(8,128)S(1)}, f32[64,128]{1,0:T(8,128)}, u32[]{:S(2)}) copy-start(f32[64,128]{1,0:T(8,128)} %constant.8.clone.select_ref) | copy-start | bytes 98308
where the time goes:
time: 73.6 us; the launch traced here: 72.9 us
  blocking collectives  21.1 us (29%)
  waiting for transfers between devices  18 us (24%)
  Pallas kernels  15.8 us (21%)
  starting transfers between devices  11 us (15%)
  local copies, waits for them, and re-layouts  6.89 us (9%)
    all_to_all x2, blocking collectives, exchange(): return lax.all_to_all(blocks, 'tm', split_axis=0, concat_axis=0, tiled=True)  21.1 us
    all_to_all x2, waiting for transfers between devices, exchange(): return lax.all_to_all(blocks, 'tm', split_axis=0, concat_axis=0, tiled=True)  18 us
    all_to_all x2, starting transfers between devices, exchange(): return lax.all_to_all(blocks, 'tm', split_axis=0, concat_axis=0, tiled=True)  11 us
    unnamed x28, local copies, waits for them, and re-layouts  6.89 us
    pallas_call x1, Pallas kernels, strips_body(): pl.pallas_call(middle_kernel, out_shape=(f32(strips, blocks, span), f32(2...  5.88 us
    pallas_call x1, Pallas kernels, strips_body(): pl.pallas_call(frame_kernel, grid=(width // rows,), out_shape=f32(strips,...  4.98 us
    pallas_call x1, Pallas kernels, strips_body(): pl.pallas_call(last_kernel, out_shape=f32(frames, strip, length), in_spec...  1.57 us
  transfers between devices with their start and end apart: 2, of which 2 were waited for; matrix products, arithmetic and copies ran while one was open for 0% of the time, Pallas kernels for 3%

commit v1 on v0

--- a/solution.py
+++ b/solution.py
@@ -155,16 +155,14 @@
     return lax.broadcasted_iota(jnp.int32, shape, dim)
 
 
-def wide_tables(length):
+def wide_table(length):
     indices = np.arange(length, dtype=np.int32)
     phases = indices[:, None] * indices[None, :] % length
     angles = phases.astype(np.float32) * np.float32(2.0 * math.pi / length)
     norm_scale = np.float32(1.0 / math.sqrt(length))
     cosine = (np.cos(angles) * norm_scale).astype(ml_dtypes.bfloat16)
     sine = (np.sin(angles) * norm_scale).astype(ml_dtypes.bfloat16)
-    ahead = np.block([[cosine, -sine], [sine, cosine]])
-    back = np.block([[cosine, sine], [-sine, cosine]])
-    return ahead, back
+    return np.block([[cosine, -sine], [sine, cosine]])
 
 
 def pair_list(frames):
@@ -192,84 +190,106 @@
     return jnp.sum(x.reshape(rows // 8, 8, length), axis=0)
 
 
-def pack_kernel(offsets_ref, start_ref, lines_ref, out_ref):
+def frame_kernel(
+    offsets_hbm, start_hbm, sens_hbm, data_hbm, lines_hbm, table_hbm, out_ref,
+    offsets_ref, start_ref, sens_ref, data_ref, lines_ref, table_ref, grad, left, right, sems, chunk_sems,
+):
+    chunks, coils, _, rows, length = sens_ref.shape
+    start_copy, lines_copy, table_copy, offsets_copy = (
+        pltpu.make_async_copy(source, target, sems.at[k])
+        for k, (source, target) in enumerate(
+            ((start_hbm, start_ref), (lines_hbm, lines_ref), (table_hbm, table_ref), (offsets_hbm, offsets_ref))
+        )
+    )
+    sens_copy = [
+        pltpu.make_async_copy(sens_hbm.at[:, :, pl.ds(i * rows, rows), :], sens_ref.at[i], chunk_sems.at[0, i])
+        for i in range(chunks)
+    ]
+    data_copy = [
+        pltpu.make_async_copy(data_hbm.at[0, :, :, pl.ds(i * rows, rows), :], data_ref.at[i], chunk_sems.at[1, i])
+        for i in range(chunks)
+    ]
+    start_copy.start()
+    sens_copy[0].start()
+    table_copy.start()
+    data_copy[0].start()
+    lines_copy.start()
+    offsets_copy.start()
+    for i in range(1, chunks):
+        sens_copy[i].start()
+        data_copy[i].start()
+    num = jnp.zeros((8, length), jnp.float32)
+    den = jnp.zeros((8, length), jnp.float32)
+
+    def coil_image(i, a, b):
+        for c in range(coils):
+            sr = sens_ref[i, c, 0].astype(jnp.float32)
+            si = sens_ref[i, c, 1].astype(jnp.float32)
+            at = slice(c * rows, (c + 1) * rows)
+            left[i, at, :length] = (sr * a - si * b).astype(jnp.bfloat16)
+            left[i, at, length:] = (sr * b + si * a).astype(jnp.bfloat16)
+
+    start_copy.wait()
+    for i in range(chunks):
+        place = slice(i * rows, (i + 1) * rows)
+        sens_copy[i].wait()
+        coil_image(i, start_ref[0, 0, place], start_ref[0, 1, place])
+        if i == 0:
+            table_copy.wait()
+        spec = mxu(left[i], table_ref[...])
+        if i == 0:
+            lines_copy.wait()
+        weight = lines_ref[0].astype(jnp.float32)
+        data_copy[i].wait()
+        for c in range(coils):
+            at = slice(c * rows, (c + 1) * rows)
+            w = weight[c : c + 1]
+            right[i, at, :length] = (w * (spec[at, :length] - data_ref[i, c, 0].astype(jnp.float32))).astype(jnp.bfloat16)
+            right[i, at, length:] = (w * (data_ref[i, c, 1].astype(jnp.float32) - spec[at, length:])).astype(jnp.bfloat16)
+        home = mxu(right[i], table_ref[...])
+        gr = jnp.zeros((rows, length), jnp.float32)
+        gi = jnp.zeros((rows, length), jnp.float32)
+        for c in range(coils):
+            sr = sens_ref[i, c, 0].astype(jnp.float32)
+            si = sens_ref[i, c, 1].astype(jnp.float32)
+            at = slice(c * rows, (c + 1) * rows)
+            br, bi = home[at, :length], home[at, length:]
+            gr = gr + (sr * br - si * bi)
+            gi = gi - (sr * bi + si * br)
+        grad[0, place, :] = gr
+        grad[1, place, :] = gi
+        num = num + fold(gr * gr + gi * gi)
+        coil_image(i, gr, gi)
+        probe = mxu(left[i], table_ref[...])
+        for c in range(coils):
+            at = slice(c * rows, (c + 1) * rows)
+            pr, pi = probe[at, :length], probe[at, length:]
+            den = den + weight[c : c + 1] * fold(pr * pr + pi * pi)
+
+    strips = out_ref.shape[0]
+    halves = length // LANES
+    strip = 2 * BS
+    weight = lines_ref[0].astype(jnp.float32)
+    numer = jnp.sum(jnp.sum(num, axis=0, keepdims=True), axis=1, keepdims=True)
+    denom = jnp.sum(jnp.sum(den, axis=0, keepdims=True), axis=1, keepdims=True)
+    sums = jnp.where(iota((8, LANES), 0) == 0, numer, denom)
+    offsets_copy.wait()
     shift = offsets_ref[0, 0]
-    strips = out_ref.shape[0]
-    for part in range(2):
-        rolled = pltpu.roll(start_ref[0, part], shift, 0)
-        out_ref[:, part * BS : (part + 1) * BS, :] = rolled.reshape(strips, BS, rolled.shape[1])
-    lines = lines_ref[0].astype(jnp.float32)
-    coils = lines.shape[0]
-    for strip in range(strips):
-        out_ref[strip, 2 * BS : 2 * BS + coils, :] = lines
-
-
-def frame_kernel(offsets_ref, start_ref, sens_ref, data_ref, lines_ref, ahead_ref, back_ref, out_ref, grad, num, den, left, right):
-    step = pl.program_id(0)
-    coils, _, rows, length = sens_ref.shape
-    weight = lines_ref[0].astype(jnp.float32)
-
-    @pl.when(step == 0)
-    def _():
-        num[...] = jnp.zeros_like(num)
-        den[...] = jnp.zeros_like(den)
-
-    def coil_image(a, b):
-        for c in range(coils):
-            sr = sens_ref[c, 0].astype(jnp.float32)
-            si = sens_ref[c, 1].astype(jnp.float32)
-            at = slice(c * rows, (c + 1) * rows)
-            left[at, :length] = (sr * a - si * b).astype(jnp.bfloat16)
-            left[at, length:] = (sr * b + si * a).astype(jnp.bfloat16)
-
-    coil_image(start_ref[0, 0], start_ref[0, 1])
-    spec = mxu(left[...], ahead_ref[...])
-    for c in range(coils):
-        at = slice(c * rows, (c + 1) * rows)
-        w = weight[c : c + 1]
-        right[at, :length] = (w * (spec[at, :length] - data_ref[0, c, 0].astype(jnp.float32))).astype(jnp.bfloat16)
-        right[at, length:] = (w * (spec[at, length:] - data_ref[0, c, 1].astype(jnp.float32))).astype(jnp.bfloat16)
-    home = mxu(right[...], back_ref[...])
-    gr = jnp.zeros((rows, length), jnp.float32)
-    gi = jnp.zeros((rows, length), jnp.float32)
-    for c in range(coils):
-        sr = sens_ref[c, 0].astype(jnp.float32)
-        si = sens_ref[c, 1].astype(jnp.float32)
-        at = slice(c * rows, (c + 1) * rows)
-        br, bi = home[at, :length], home[at, length:]
-        gr = gr + (sr * br + si * bi)
-        gi = gi + (sr * bi - si * br)
-    where = pl.ds(pl.multiple_of(step * rows, rows), rows)
-    grad[0, where, :] = gr
-    grad[1, where, :] = gi
-    num[...] += fold(gr * gr + gi * gi)
-    coil_image(gr, gi)
-    probe = mxu(left[...], ahead_ref[...])
-    total = jnp.zeros((8, length), jnp.float32)
-    for c in range(coils):
-        at = slice(c * rows, (c + 1) * rows)
-        pr, pi = probe[at, :length], probe[at, length:]
-        total = total + weight[c : c + 1] * fold(pr * pr + pi * pi)
-    den[...] += total
-
-    @pl.when(step == pl.num_programs(0) - 1)
-    def _():
-        shift = offsets_ref[0, 0]
-        strips = out_ref.shape[0]
+    for kind, image in enumerate((start_ref.at[0], grad)):
         for part in range(2):
-            rolled = pltpu.roll(grad[part], shift, 0)
-            out_ref[:, part * BS : (part + 1) * BS, :] = rolled.reshape(strips, BS, length)
-        sums = jnp.where(
-            iota((8, length), 0) == 0,
-            jnp.sum(num[...], axis=0, keepdims=True),
-            jnp.sum(den[...], axis=0, keepdims=True),
-        )
-        for strip in range(strips):
-            out_ref[strip, 2 * BS : 2 * BS + 8, :] = sums
+            rolled = pltpu.roll(image[part], shift, 0)
+            for half in range(halves):
+                base = (kind * halves + half) * strip + part * BS
+                out_ref[:, base : base + BS, :] = rolled[:, half * LANES : (half + 1) * LANES].reshape(strips, BS, LANES)
+    for target in range(strips):
+        for half in range(halves):
+            base = 2 * halves * strip + half * coils
+            out_ref[target, base : base + coils, :] = weight[:, half * LANES : (half + 1) * LANES]
+        base = 2 * halves * strip + halves * coils
+        out_ref[target, base : base + 8, :] = sums
 
 
 def strip_kernel(offsets_ref, sens_ref, out_ref, both, sems):
-    axis = out_ref.shape
     coils, _, width, length = sens_ref.shape
     strips = width // BS
     me = lax.axis_index("tm")
@@ -330,24 +350,37 @@
 
 
 def middle_kernel(
-    offsets_ref, image_ref, first_ref, sens_ref, ahead_ref, back_ref,
+    offsets_ref, mail_ref, sens_ref, table_ref,
     out_ref, own_ref, est_ref, grad_ref,
     terms, held, other, spread, left, right,
 ):
-    frames = image_ref.shape[0]
+    frames = mail_ref.shape[0]
     coils, _, _, length = sens_ref.shape
     pairs = pair_list(frames)
     strip = 2 * BS
-    numer = jnp.zeros((1, length), jnp.float32)
-    denom = jnp.zeros((1, length), jnp.float32)
-    for f in range(frames):
-        numer = numer + first_ref[f, strip : strip + 1, :]
-        denom = denom + first_ref[f, strip + 1 : strip + 2, :]
-    numer = jnp.sum(numer, axis=1, keepdims=True)
-    denom = jnp.sum(denom, axis=1, keepdims=True)
+    halves = length // LANES
+
+    def mail(f, kind, first, rows):
+        return jnp.concatenate(
+            [
+                mail_ref[f, (kind * halves + half) * strip + first : (kind * halves + half) * strip + first + rows, :]
+                for half in range(halves)
+            ],
+            axis=1,
+        )
+
+    def mask(f):
+        base = 2 * halves * strip
+        return jnp.concatenate(
+            [mail_ref[f, base + half * coils : base + (half + 1) * coils, :] for half in range(halves)], axis=1
+        )
+
+    place = 2 * halves * strip + halves * coils
+    numer = sum(mail_ref[f, place : place + 1, :1] for f in range(frames))
+    denom = sum(mail_ref[f, place + 1 : place + 2, :1] for f in range(frames))
     step = numer / (denom + epsilon)
     for f in range(frames):
-        est_ref[f] = image_ref[f, :strip, :] - step * first_ref[f, :strip, :]
+        est_ref[f] = mail(f, 0, 0, strip) - step * mail(f, 1, 0, strip)
     for f, g in pairs:
         tile = fold(est_ref[f] * est_ref[g])
         for place in {f * frames + g, g * frames + f}:
@@ -373,53 +406,51 @@
 
     num = jnp.zeros((8, length), jnp.float32)
     den = jnp.zeros((8, length), jnp.float32)
-    group = left.shape[0] // (coils * BS)
-
-    def coil_image(values):
+    group = left.shape[1] // (coils * BS)
+
+    def coil_image(index, values):
         for k, (a, b) in enumerate(values):
             for c in range(coils):
                 sr, si = sens_ref[c, 0], sens_ref[c, 1]
                 at = slice((k * coils + c) * BS, (k * coils + c + 1) * BS)
-                left[at, :length] = (sr * a - si * b).astype(jnp.bfloat16)
-                left[at, length:] = (sr * b + si * a).astype(jnp.bfloat16)
+                left[index, at, :length] = (sr * a - si * b).astype(jnp.bfloat16)
+                left[index, at, length:] = (sr * b + si * a).astype(jnp.bfloat16)
 
     def passes(index, carry):
         num, den = carry
         at_frame = [index * group + k for k in range(group)]
         coil_image(
+            index,
             [
-                (
-                    est_ref[f, :BS, :] - image_ref[f, :BS, :],
-                    est_ref[f, BS:strip, :] - image_ref[f, BS:strip, :],
-                )
+                (est_ref[f, :BS, :] - mail(f, 0, 0, BS), est_ref[f, BS:strip, :] - mail(f, 0, BS, BS))
                 for f in at_frame
-            ]
+            ],
         )
-        weights = [image_ref[f, strip : strip + coils, :] for f in at_frame]
-        spec = mxu(left[...], ahead_ref[...])
+        weights = [mask(f) for f in at_frame]
+        spec = mxu(left[index], table_ref[...])
         for k in range(group):
             for c in range(coils):
                 at = slice((k * coils + c) * BS, (k * coils + c + 1) * BS)
                 w = weights[k][c : c + 1]
-                right[at, :length] = (w * spec[at, :length]).astype(jnp.bfloat16)
-                right[at, length:] = (w * spec[at, length:]).astype(jnp.bfloat16)
-        home = mxu(right[...], back_ref[...])
+                right[index, at, :length] = (w * spec[at, :length]).astype(jnp.bfloat16)
+                right[index, at, length:] = (-w * spec[at, length:]).astype(jnp.bfloat16)
+        home = mxu(right[index], table_ref[...])
         values = []
         for k, f in enumerate(at_frame):
-            gr = first_ref[f, :BS, :]
-            gi = first_ref[f, BS:strip, :]
+            gr = mail(f, 1, 0, BS)
+            gi = mail(f, 1, BS, BS)
             for c in range(coils):
                 at = slice((k * coils + c) * BS, (k * coils + c + 1) * BS)
                 sr, si = sens_ref[c, 0], sens_ref[c, 1]
                 br, bi = home[at, :length], home[at, length:]
-                gr = gr + (sr * br + si * bi)
-                gi = gi + (sr * bi - si * br)
+                gr = gr + (sr * br - si * bi)
+                gi = gi - (sr * bi + si * br)
             grad_ref[f, :BS, :] = gr
             grad_ref[f, BS:strip, :] = gi
             num = num + fold(gr * gr + gi * gi)
             values.append((gr, gi))
-        coil_image(values)
-        probe = mxu(left[...], ahead_ref[...])
+        coil_image(index, values)
+        probe = mxu(left[index], table_ref[...])
         for k in range(group):
             for c in range(coils):
                 at = slice((k * coils + c) * BS, (k * coils + c + 1) * BS)
@@ -427,7 +458,8 @@
                 den = den + weights[k][c : c + 1] * fold(pr * pr + pi * pi)
         return num, den
 
-    num, den = lax.fori_loop(0, frames // group, passes, (num, den))
+    for index in range(frames // group):
+        num, den = passes(index, (num, den))
     numer = jnp.sum(jnp.sum(num, axis=0, keepdims=True), axis=1, keepdims=True)
     denom = jnp.sum(jnp.sum(den, axis=0, keepdims=True), axis=1, keepdims=True)
 
@@ -534,6 +566,10 @@
     return pl.BlockSpec(memory_space=pltpu.VMEM)
 
 
+def hbm():
+    return pl.BlockSpec(memory_space=pltpu.HBM)
+
+
 def smem():
     return pl.BlockSpec(memory_space=pltpu.SMEM)
 
@@ -546,8 +582,8 @@
     return lax.all_to_all(blocks, "tm", split_axis=0, concat_axis=0, tiled=True)
 
 
-def params():
-    return pltpu.CompilerParams(vmem_limit_bytes=32 * 1024 * 1024)
+def params(mebibytes=16):
+    return pltpu.CompilerParams(vmem_limit_bytes=mebibytes * 1024 * 1024)
 
 
 def strips_body(start_image, sensitivity, kspace, sampled, offsets):
@@ -555,52 +591,41 @@
     coils = sensitivity.shape[0]
     strips = width // BS
     frames = strips
-    ahead, back = (jnp.asarray(table) for table in wide_tables(length))
+    table = jnp.asarray(wide_table(length))
     strip = 2 * BS
     span = LANES
     blocks = length // BS
-
-    packed = pl.pallas_call(
-        pack_kernel,
-        out_shape=f32(strips, strip + coils, length),
-        in_specs=[smem(), vmem(), vmem()],
+    halves = length // LANES
+
+    rows = 2 * BS
+    chunks = width // rows
+    mail = pl.pallas_call(
+        frame_kernel,
+        out_shape=f32(strips, halves * (2 * strip + coils) + 8, LANES),
+        in_specs=[hbm()] * 6,
         out_specs=vmem(),
-        compiler_params=params(),
-        cost_estimate=pl.CostEstimate(flops=10**6, bytes_accessed=10**6, transcendentals=0),
-    )(offsets, start_image, sampled)
-    image = exchange(packed)
-
-    rows = 2 * BS
-    first = pl.pallas_call(
-        frame_kernel,
-        grid=(width // rows,),
-        out_shape=f32(strips, strip + 8, length),
-        in_specs=[
-            smem(),
-            pl.BlockSpec((1, 2, rows, length), lambda i: (0, 0, i, 0)),
-            pl.BlockSpec((coils, 2, rows, length), lambda i: (0, 0, i, 0)),
-            pl.BlockSpec((1, coils, 2, rows, length), lambda i: (0, 0, 0, i, 0)),
-            pl.BlockSpec((1, coils, length), lambda i: (0, 0, 0)),
-            vmem(),
-            vmem(),
+        scratch_shapes=[
+            pltpu.SMEM(offsets.shape, jnp.int32),
+            pltpu.VMEM(start_image.shape, jnp.float32),
+            pltpu.VMEM((chunks, coils, 2, rows, length), jnp.bfloat16),
+            pltpu.VMEM((chunks, coils, 2, rows, length), jnp.bfloat16),
+            pltpu.VMEM(sampled.shape, jnp.int32),
+            pltpu.VMEM(table.shape, jnp.bfloat16),
+            pltpu.VMEM((2, width, length), jnp.float32),
+            pltpu.VMEM((chunks, coils * rows, 2 * length), jnp.bfloat16),
+            pltpu.VMEM((chunks, coils * rows, 2 * length), jnp.bfloat16),
+            pltpu.SemaphoreType.DMA((4,)),
+            pltpu.SemaphoreType.DMA((2, chunks)),
         ],
-        out_specs=pl.BlockSpec((strips, strip + 8, length), lambda i: (0, 0, 0)),
-        scratch_shapes=[
-            pltpu.VMEM((2, width, length), jnp.float32),
-            pltpu.VMEM((8, length), jnp.float32),
-            pltpu.VMEM((8, length), jnp.float32),
-            pltpu.VMEM((coils * rows, 2 * length), jnp.bfloat16),
-            pltpu.VMEM((coils * rows, 2 * length), jnp.bfloat16),
-        ],
-        compiler_params=params(),
+        compiler_params=params(60),
         cost_estimate=pl.CostEstimate(flops=24 * coils * width * length * length, bytes_accessed=4 * 10**6, transcendentals=0),
-    )(offsets, start_image, sensitivity, kspace, sampled, ahead, back)
-    first = exchange(first)
+    )(offsets, start_image, sensitivity, kspace, sampled, table)
+    mail = exchange(mail)
 
     sens = pl.pallas_call(
         strip_kernel,
         out_shape=f32(coils, 2, BS, length),
-        in_specs=[smem(), pl.BlockSpec(memory_space=pl.ANY)],
+        in_specs=[smem(), hbm()],
         out_specs=vmem(),
         scratch_shapes=[pltpu.VMEM((2, coils, 2, BS, length), jnp.bfloat16), pltpu.SemaphoreType.DMA((2,))],
         compiler_params=params(),
@@ -617,19 +642,19 @@
             f32(frames, strip, length),
             f32(frames, strip, length),
         ),
-        in_specs=[smem()] + [vmem()] * 5,
+        in_specs=[smem()] + [vmem()] * 3,
         out_specs=(vmem(),) * 4,
         scratch_shapes=[
             pltpu.VMEM((length // LANES, 2 * span * 8, LANES), jnp.float32),
             pltpu.VMEM((count, LANES), jnp.float32),
             pltpu.VMEM((count, LANES), jnp.float32),
             pltpu.VMEM((count, length), jnp.float32),
-            pltpu.VMEM((group * coils * BS, 2 * length), jnp.bfloat16),
-            pltpu.VMEM((group * coils * BS, 2 * length), jnp.bfloat16),
+            pltpu.VMEM((frames // group, group * coils * BS, 2 * length), jnp.bfloat16),
+            pltpu.VMEM((frames // group, group * coils * BS, 2 * length), jnp.bfloat16),
         ],
         compiler_params=params(),
         cost_estimate=pl.CostEstimate(flops=24 * coils * width * length * length, bytes_accessed=4 * 10**6, transcendentals=0),
-    )(offsets, image, first, sens, ahead, back)
+    )(offsets, mail, sens, table)
     heard = exchange(sent)
 
     returned = pl.pallas_call(

time: 73.6 us -> 59.8 us (0.81)
  local copies, waits for them, and re-layouts: 6.89 us -> 0.02 us
  starting transfers between devices: 11 us -> 7.39 us
  waiting for transfers between devices: 18 us -> 15.9 us
  Pallas kernels: 15.8 us -> 14.9 us
    unnamed x28 -> x8, local copies, waits for them, and re-layouts: 6.89 us -> 0.02 us
    all_to_all x2 -> x1, starting transfers between devices: 11 us -> 7.39 us  [exchange(): return lax.all_to_all(blocks, 'tm', split_axis=0, concat_axis=0, tiled=True)]
    all_to_all x2 -> x1, waiting for transfers between devices: 18 us -> 15.9 us  [exchange(): return lax.all_to_all(blocks, 'tm', split_axis=0, concat_axis=0, tiled=True)]
    pallas_call x1, Pallas kernels: 5.88 us -> 4.94 us  [strips_body(): pl.pallas_call(middle_kernel, out_shape=(f32(strips, blocks, span), f32(2...]
    pallas_call x2 -> x1, Pallas kernels: 6.32 us -> 6.37 us  [strips_body(): pl.pallas_call(frame_kernel, out_shape=f32(strips, halves * (2 * strip +...]
  transfers between devices with their start and end apart: 2 -> 1, of which waited for: 2 -> 1; matrix products, arithmetic and copies ran while one was open for 0% -> 0% of each run, Pallas kernels for 3% -> 1%
where the time goes in v1:
time: 59.8 us; the launch traced here: 59.4 us
  blocking collectives  21.1 us (35%)
  waiting for transfers between devices  15.9 us (27%)
  Pallas kernels  14.9 us (25%)
  starting transfers between devices  7.39 us (12%)
    all_to_all x2, blocking collectives, exchange(): return lax.all_to_all(blocks, 'tm', split_axis=0, concat_axis=0, tiled=True)  21.1 us
    all_to_all x1, waiting for transfers between devices, exchange(): return lax.all_to_all(blocks, 'tm', split_axis=0, concat_axis=0, tiled=True)  15.9 us
    all_to_all x1, starting transfers between devices, exchange(): return lax.all_to_all(blocks, 'tm', split_axis=0, concat_axis=0, tiled=True)  7.39 us
    pallas_call x1, Pallas kernels, strips_body(): pl.pallas_call(frame_kernel, out_shape=f32(strips, halves * (2 * strip +...  6.37 us
    pallas_call x1, Pallas kernels, strips_body(): pl.pallas_call(middle_kernel, out_shape=(f32(strips, blocks, span), f32(2...  4.94 us
    pallas_call x1, Pallas kernels, strips_body(): pl.pallas_call(last_kernel, out_shape=f32(frames, strip, length), in_spec...  1.57 us
    pallas_call x1, Pallas kernels, strips_body(): pl.pallas_call(place_kernel, out_shape=f32(1, 2, width, length), in_specs...  1.32 us
  transfers between devices with their start and end apart: 1, of which 1 were waited for; matrix products, arithmetic and copies ran while one was open for 0% of the time, Pallas kernels for 1%

profile of v1, /device:TPU:0, one launch (start us, length us, event | category | flops | bytes accessed | tf_op | source)
XLA Modules:
  0.0 59.4 jit_solution(1715705736659329630)
XLA Ops:
  0.0 6.4 %shard_map.73 = f32[8,152,128]{2,1,0:T(8,128)} custom-call(s32[2,2]{1,0:T(2,128)} %offsets_ref.7, f32[1,2,128,256]{3,2,1,0:T(8,128)} %start_hbm.1, bf16[8,2,128,256]{3,2,1,0:T(8,128)(2,1)} %sens_ref.1, bf16[1,8,2,128,256]{4,3,2,1,0:T(8,128)(2,1)} %data_hbm.1, s32[1,8,256]{2,1,0:T(8,128)} %lines_hbm.1, bf16[512,512]{1,0:T(8,128)(2,1)} %constant.4.clone.table_hbm.table_ref), custom_call_target="tpu_custom_call" | custom-call | flops 1610612736 | bytes 4000000 | tf_op jit(solution)/shard_map/pallas_call | solution.py:602
  6.4 0.0 copy-start
  6.4 0.0 copy-start.2
  6.4 7.4 %all-to-all-start = ((f32[8,152,128]{2,1,0:T(8,128)}), f32[8,152,128]{2,1,0:T(8,128)S(1)}, u32[]{:S(2)}, u32[]{:S(2)}) async-start(f32[8,152,128]{2,1,0:T(8,128)} %shard_map.73), calls=%async_computation | async-start | bytes 1245184 | tf_op jit(solution)/shard_map/all_to_all | solution.py:582
  13.8 0.0 copy-done
  13.8 0.0 copy-done.2
  13.8 0.0 copy-start.3
  13.8 0.7 %shard_map.74.sens_ref = f32[8,2,16,256]{3,2,1,0:T(8,128)S(1)} custom-call(s32[2,2]{1,0:T(2,128)S(1)} %copy-done.2, bf16[8,2,128,256]{3,2,1,0:T(8,128)(2,1)S(1)} %copy-done), custom_call_target="tpu_custom_call" | custom-call | flops 1000000 | bytes 1000000 | tf_op jit(solution)/shard_map/pallas_call | solution.py:625
  14.5 15.9 %all-to-all-done.mail_ref = f32[8,152,128]{2,1,0:T(8,128)S(1)} async-done(((f32[8,152,128]{2,1,0:T(8,128)}), f32[8,152,128]{2,1,0:T(8,128)S(1)}, u32[]{:S(2)}, u32[]{:S(2)}) %all-to-all-start) | async-done | bytes 622624 | tf_op jit(solution)/shard_map/all_to_all | solution.py:582
  30.4 0.0 copy-done.3
  30.4 4.9 %shard_map.75 = (f32[8,16,128]{2,1,0:T(8,128)S(1)}, f32[32,128]{1,0:T(8,128)S(1)}, f32[8,32,256]{2,1,0:T(8,128)S(1)}, f32[8,32,256]{2,1,0:T(8,128)S(1)}) custom-call(s32[2,2]{1,0:T(2,128)S(1)} %copy-done.2, f32[8,152,128]{2,1,0:T(8,128)S(1)} %all-to-all-done.mail_ref, f32[8,2,16,256]{3,2,1,0:T(8,128)S(1)} %shard_map.74.sens_ref, bf16[512,512]{1,0:T(8,128)(2,1)S(1)} %copy-done.3), custom_call_target="tpu_custom_call" | custom-call | flops 1610612736 | bytes 4000000 | tf_op jit(solution)/shard_map/pallas_call | solution.py:637
  35.4 0.0 copy-start.1
  35.4 10.5 %all_to_all.15.heard_ref = f32[8,16,128]{2,1,0:T(8,128)S(1)} all-to-all(f32[8,16,128]{2,1,0:T(8,128)S(1)} %get-tuple-element.10), channel_id=1, replica_groups=mesh['tm'=8,'cuts'=4] {'tm'}, dimensions={0} | all-to-all | bytes 131072 | tf_op jit(solution)/shard_map/all_to_all | solution.py:582
  45.9 0.0 copy-done.1
  45.9 1.6 %shard_map.76 = f32[8,32,256]{2,1,0:T(8,128)S(1)} custom-call(s32[2,2]{1,0:T(2,128)S(1)} %copy-done.2, f32[32,128]{1,0:T(8,128)S(1)} %get-tuple-element.9.own_ref, f32[8,16,128]{2,1,0:T(8,128)S(1)} %all_to_all.15.heard_ref, f32[8,32,256]{2,1,0:T(8,128)S(1)} %get-tuple-element.11.est_ref, f32[8,32,256]{2,1,0:T(8,128)S(1)} %get-tuple-element.12.grad_ref, ...), custom_call_target="tpu_custom_call" | custom-call | tf_op jit(solution)/shard_map/pallas_call | solution.py:660
  47.5 10.6 %all_to_all.16.strips_ref = f32[8,32,256]{2,1,0:T(8,128)S(1)} all-to-all(f32[8,32,256]{2,1,0:T(8,128)S(1)} %shard_map.76), channel_id=1, replica_groups=mesh['tm'=8,'cuts'=4] {'tm'}, dimensions={0} | all-to-all | bytes 524288 | tf_op jit(solution)/shard_map/all_to_all | solution.py:582
  58.1 1.3 %shard_map.77 = f32[1,2,128,256]{3,2,1,0:T(8,128)} custom-call(s32[2,2]{1,0:T(2,128)S(1)} %copy-done.2, f32[8,32,256]{2,1,0:T(8,128)S(1)} %all_to_all.16.strips_ref), custom_call_target="tpu_custom_call" | custom-call | tf_op jit(solution)/shard_map/pallas_call | solution.py:675
Async XLA Ops:
  6.4 7.4 %copy-start = (bf16[8,2,128,256]{3,2,1,0:T(8,128)(2,1)S(1)}, bf16[8,2,128,256]{3,2,1,0:T(8,128)(2,1)}, u32[]{:S(2)}) copy-start(bf16[8,2,128,256]{3,2,1,0:T(8,128)(2,1)} %sens_ref.1) | copy-start | bytes 3145732
  6.4 7.4 %copy-start.2 = (s32[2,2]{1,0:T(2,128)S(1)}, s32[2,2]{1,0:T(2,128)}, u32[]{:S(2)}) copy-start(s32[2,2]{1,0:T(2,128)} %offsets_ref.7) | copy-start | bytes 52
  6.4 24.0 %all-to-all-start = ((f32[8,152,128]{2,1,0:T(8,128)}), f32[8,152,128]{2,1,0:T(8,128)S(1)}, u32[]{:S(2)}, u32[]{:S(2)}) async-start(f32[8,152,128]{2,1,0:T(8,128)} %shard_map.73), calls=%async_computation | async-start | bytes 1245184 | tf_op jit(solution)/shard_map/all_to_all | solution.py:582
  13.8 16.6 %copy-start.3 = (bf16[512,512]{1,0:T(8,128)(2,1)S(1)}, bf16[512,512]{1,0:T(8,128)(2,1)}, u32[]{:S(2)}) copy-start(bf16[512,512]{1,0:T(8,128)(2,1)} %constant.4.clone.table_hbm.table_ref) | copy-start | bytes 1572868
  35.4 10.5 %copy-start.1 = (f32[64,128]{1,0:T(8,128)S(1)}, f32[64,128]{1,0:T(8,128)}, u32[]{:S(2)}) copy-start(f32[64,128]{1,0:T(8,128)} %constant.5.clone.select_ref) | copy-start | bytes 98308

commit v2 on v1

--- a/solution.py
+++ b/solution.py
@@ -177,8 +177,26 @@
     return table
 
 
-def exact_dot(a, b, dims=(((1,), (0,)), ((), ()))):
-    return lax.dot_general(a, b, dims, precision=lax.Precision.HIGHEST, preferred_element_type=jnp.float32)
+def pieces(x):
+    first = x.astype(jnp.bfloat16)
+    rest = x - first.astype(jnp.float32)
+    second = rest.astype(jnp.bfloat16)
+    third = (rest - second.astype(jnp.float32)).astype(jnp.bfloat16)
+    return jnp.concatenate([first, second, third], axis=0)
+
+
+def pick(x, ones):
+    rows = x.shape[0]
+    out = mxu(pieces(x), ones.astype(jnp.bfloat16))
+    return out[:rows] + out[rows : 2 * rows] + out[2 * rows :]
+
+
+def pick_rows(ones, x):
+    rows = x.shape[0]
+    out = lax.dot_general(
+        ones.astype(jnp.bfloat16), pieces(x), (((1,), (1,)), ((), ())), preferred_element_type=jnp.float32
+    )
+    return out[:, :rows] + out[:, rows : 2 * rows] + out[:, 2 * rows :]
 
 
 def mxu(a, b):
@@ -191,7 +209,7 @@
 
 
 def frame_kernel(
-    offsets_hbm, start_hbm, sens_hbm, data_hbm, lines_hbm, table_hbm, out_ref,
+    offsets_hbm, start_hbm, sens_hbm, data_hbm, lines_hbm, table_hbm, out_ref, strip_ref, copied_ref,
     offsets_ref, start_ref, sens_ref, data_ref, lines_ref, table_ref, grad, left, right, sems, chunk_sems,
 ):
     chunks, coils, _, rows, length = sens_ref.shape
@@ -209,17 +227,16 @@
         pltpu.make_async_copy(data_hbm.at[0, :, :, pl.ds(i * rows, rows), :], data_ref.at[i], chunk_sems.at[1, i])
         for i in range(chunks)
     ]
+    offsets_copy.start()
     start_copy.start()
+    lines_copy.start()
     sens_copy[0].start()
     table_copy.start()
-    data_copy[0].start()
-    lines_copy.start()
-    offsets_copy.start()
-    for i in range(1, chunks):
-        sens_copy[i].start()
-        data_copy[i].start()
-    num = jnp.zeros((8, length), jnp.float32)
-    den = jnp.zeros((8, length), jnp.float32)
+    for copy in sens_copy[1:] + data_copy:
+        copy.start()
+    strips = out_ref.shape[0]
+    halves = length // LANES
+    strip = 2 * BS
 
     def coil_image(i, a, b):
         for c in range(coils):
@@ -229,86 +246,85 @@
             left[i, at, :length] = (sr * a - si * b).astype(jnp.bfloat16)
             left[i, at, length:] = (sr * b + si * a).astype(jnp.bfloat16)
 
+    def post(kind, image):
+        shift = offsets_ref[0, 0]
+        for part in range(2):
+            rolled = pltpu.roll(image[part], shift, 0)
+            for half in range(halves):
+                base = (kind * halves + half) * strip + part * BS
+                out_ref[:, base : base + BS, :] = rolled[:, half * LANES : (half + 1) * LANES].reshape(strips, BS, LANES)
+
+    offsets_copy.wait()
     start_copy.wait()
+    lines_copy.wait()
+    copied = jnp.zeros(copied_ref.shape, jnp.int32)
+    for k in range(copied.shape[0]):
+        for axis in range(copied.shape[1]):
+            here = (iota(copied.shape, 0) == k) & (iota(copied.shape, 1) == axis)
+            copied = jnp.where(here, offsets_ref[k, axis], copied)
+    copied_ref[...] = copied
+    weight = lines_ref[0].astype(jnp.float32)
+    post(0, start_ref.at[0])
+    for target in range(strips):
+        for half in range(halves):
+            base = 2 * halves * strip + half * coils
+            out_ref[target, base : base + coils, :] = weight[:, half * LANES : (half + 1) * LANES]
+    spec = []
     for i in range(chunks):
-        place = slice(i * rows, (i + 1) * rows)
         sens_copy[i].wait()
-        coil_image(i, start_ref[0, 0, place], start_ref[0, 1, place])
+        coil_image(i, start_ref[0, 0, i * rows : (i + 1) * rows], start_ref[0, 1, i * rows : (i + 1) * rows])
         if i == 0:
             table_copy.wait()
-        spec = mxu(left[i], table_ref[...])
-        if i == 0:
-            lines_copy.wait()
-        weight = lines_ref[0].astype(jnp.float32)
+        spec.append(mxu(left[i], table_ref[...]))
+    me = lax.axis_index("tm")
+    each = rows // BS
+    pair = []
+    for place in (lax.rem(me + strips - 1, strips), me):
+        pair.append((place // each, pl.ds(pl.multiple_of(lax.rem(place, each) * BS, BS), BS)))
+    shift = offsets_ref[0, 0]
+    for c in range(coils):
+        for part in range(2):
+            two = jnp.concatenate([sens_ref[i, c, part, at, :] for i, at in pair], axis=0).astype(jnp.float32)
+            strip_ref[c, part] = pltpu.roll(two, shift, 0)[BS:]
+    home = []
+    for i in range(chunks):
         data_copy[i].wait()
         for c in range(coils):
             at = slice(c * rows, (c + 1) * rows)
             w = weight[c : c + 1]
-            right[i, at, :length] = (w * (spec[at, :length] - data_ref[i, c, 0].astype(jnp.float32))).astype(jnp.bfloat16)
-            right[i, at, length:] = (w * (data_ref[i, c, 1].astype(jnp.float32) - spec[at, length:])).astype(jnp.bfloat16)
-        home = mxu(right[i], table_ref[...])
+            right[i, at, :length] = (w * (spec[i][at, :length] - data_ref[i, c, 0].astype(jnp.float32))).astype(jnp.bfloat16)
+            right[i, at, length:] = (w * (data_ref[i, c, 1].astype(jnp.float32) - spec[i][at, length:])).astype(jnp.bfloat16)
+        home.append(mxu(right[i], table_ref[...]))
+    num = jnp.zeros((8, length), jnp.float32)
+    probe = []
+    for i in range(chunks):
         gr = jnp.zeros((rows, length), jnp.float32)
         gi = jnp.zeros((rows, length), jnp.float32)
         for c in range(coils):
             sr = sens_ref[i, c, 0].astype(jnp.float32)
             si = sens_ref[i, c, 1].astype(jnp.float32)
             at = slice(c * rows, (c + 1) * rows)
-            br, bi = home[at, :length], home[at, length:]
+            br, bi = home[i][at, :length], home[i][at, length:]
             gr = gr + (sr * br - si * bi)
             gi = gi - (sr * bi + si * br)
-        grad[0, place, :] = gr
-        grad[1, place, :] = gi
+        grad[0, i * rows : (i + 1) * rows, :] = gr
+        grad[1, i * rows : (i + 1) * rows, :] = gi
         num = num + fold(gr * gr + gi * gi)
         coil_image(i, gr, gi)
-        probe = mxu(left[i], table_ref[...])
+        probe.append(mxu(left[i], table_ref[...]))
+    post(1, grad)
+    den = jnp.zeros((8, length), jnp.float32)
+    for i in range(chunks):
         for c in range(coils):
             at = slice(c * rows, (c + 1) * rows)
-            pr, pi = probe[at, :length], probe[at, length:]
+            pr, pi = probe[i][at, :length], probe[i][at, length:]
             den = den + weight[c : c + 1] * fold(pr * pr + pi * pi)
-
-    strips = out_ref.shape[0]
-    halves = length // LANES
-    strip = 2 * BS
-    weight = lines_ref[0].astype(jnp.float32)
     numer = jnp.sum(jnp.sum(num, axis=0, keepdims=True), axis=1, keepdims=True)
     denom = jnp.sum(jnp.sum(den, axis=0, keepdims=True), axis=1, keepdims=True)
     sums = jnp.where(iota((8, LANES), 0) == 0, numer, denom)
-    offsets_copy.wait()
-    shift = offsets_ref[0, 0]
-    for kind, image in enumerate((start_ref.at[0], grad)):
-        for part in range(2):
-            rolled = pltpu.roll(image[part], shift, 0)
-            for half in range(halves):
-                base = (kind * halves + half) * strip + part * BS
-                out_ref[:, base : base + BS, :] = rolled[:, half * LANES : (half + 1) * LANES].reshape(strips, BS, LANES)
+    base = 2 * halves * strip + halves * coils
     for target in range(strips):
-        for half in range(halves):
-            base = 2 * halves * strip + half * coils
-            out_ref[target, base : base + coils, :] = weight[:, half * LANES : (half + 1) * LANES]
-        base = 2 * halves * strip + halves * coils
         out_ref[target, base : base + 8, :] = sums
-
-
-def strip_kernel(offsets_ref, sens_ref, out_ref, both, sems):
-    coils, _, width, length = sens_ref.shape
-    strips = width // BS
-    me = lax.axis_index("tm")
-    before = lax.rem(me + strips - 1, strips)
-    first = pltpu.make_async_copy(
-        sens_ref.at[:, :, pl.ds(pl.multiple_of(before * BS, BS), BS), :], both.at[0], sems.at[0]
-    )
-    second = pltpu.make_async_copy(
-        sens_ref.at[:, :, pl.ds(pl.multiple_of(me * BS, BS), BS), :], both.at[1], sems.at[1]
-    )
-    first.start()
-    second.start()
-    first.wait()
-    second.wait()
-    shift = offsets_ref[0, 0]
-    for c in range(coils):
-        for part in range(2):
-            rows = jnp.concatenate([both[0, c, part], both[1, c, part]], axis=0).astype(jnp.float32)
-            out_ref[c, part] = pltpu.roll(rows, shift, 0)[BS:]
 
 
 def newton_inverse(system, held, other, frames):
@@ -376,9 +392,9 @@
         )
 
     place = 2 * halves * strip + halves * coils
-    numer = sum(mail_ref[f, place : place + 1, :1] for f in range(frames))
-    denom = sum(mail_ref[f, place + 1 : place + 2, :1] for f in range(frames))
-    step = numer / (denom + epsilon)
+    totals = sum(mail_ref[f, place : place + 8, :] for f in range(frames))
+    step = totals[:1] / (totals[1:2] + epsilon)
+    step = jnp.concatenate([step] * halves, axis=1)
     for f in range(frames):
         est_ref[f] = mail(f, 0, 0, strip) - step * mail(f, 1, 0, strip)
     for f, g in pairs:
@@ -393,8 +409,8 @@
     shift = offsets_ref[0, 1]
     tall = (block_of(iota((length, LANES), 0), shift, length) == iota((length, LANES), 1)).astype(jnp.float32)
     broad = (block_of(iota((LANES, length), 1), shift, length) == iota((LANES, length), 0)).astype(jnp.float32)
-    factors = shrink_factors(exact_dot(sums, tall), held, other, frames)
-    spread[...] = exact_dot(factors, broad)
+    factors = shrink_factors(pick(sums, tall), held, other, frames)
+    spread[...] = pick(factors, broad)
     moved = [est_ref[f] for f in range(frames)]
     for f in range(frames):
         total = spread[f * frames : f * frames + 1, :] * moved[0]
@@ -416,33 +432,60 @@
                 left[index, at, :length] = (sr * a - si * b).astype(jnp.bfloat16)
                 left[index, at, length:] = (sr * b + si * a).astype(jnp.bfloat16)
 
-    def passes(index, carry):
-        num, den = carry
-        at_frame = [index * group + k for k in range(group)]
+    edge = lax.rem(offsets_ref[0, 0] - offsets_ref[1, 0] + BS, BS)
+    low = [(iota((8, length), 0) + 8 * t >= edge) for t in range(BS // 8)]
+    block = len(pairs)
+    span = out_ref.shape[2]
+
+    def rows_of(product):
+        return [
+            sum(product[p * BS + 8 * t : p * BS + 8 * t + 8] for p in range(2)) for t in range(BS // 8)
+        ]
+
+    def put(part, place, tile):
+        for half in range(length // LANES):
+            terms[half, (part * span + place) * 8 : (part * span + place) * 8 + 8, :] = tile[
+                :, half * LANES : (half + 1) * LANES
+            ]
+
+    def put_kind(kind, product_of):
+        for place, pair in enumerate(pairs):
+            rows = rows_of(product_of(*pair))
+            put(0, kind * block + place, sum(jnp.where(low[t], rows[t], 0.0) for t in range(BS // 8)))
+            put(1, kind * block + place, sum(jnp.where(low[t], 0.0, rows[t]) for t in range(BS // 8)))
+
+    groups = [range(at, at + group) for at in range(0, frames, group)]
+    weights = [mask(f) for f in range(frames)]
+    spec = []
+    for index, members in enumerate(groups):
         coil_image(
             index,
-            [
-                (est_ref[f, :BS, :] - mail(f, 0, 0, BS), est_ref[f, BS:strip, :] - mail(f, 0, BS, BS))
-                for f in at_frame
-            ],
+            [(est_ref[f, :BS, :] - mail(f, 0, 0, BS), est_ref[f, BS:strip, :] - mail(f, 0, BS, BS)) for f in members],
         )
-        weights = [mask(f) for f in at_frame]
-        spec = mxu(left[index], table_ref[...])
-        for k in range(group):
+        spec.append(mxu(left[index], table_ref[...]))
+    for part in range(2):
+        for place in range(3 * block, span):
+            put(part, place, jnp.zeros((8, length), jnp.float32))
+    put_kind(0, lambda f, g: est_ref[f] * est_ref[g])
+    home = []
+    for index, members in enumerate(groups):
+        for k, f in enumerate(members):
             for c in range(coils):
                 at = slice((k * coils + c) * BS, (k * coils + c + 1) * BS)
-                w = weights[k][c : c + 1]
-                right[index, at, :length] = (w * spec[at, :length]).astype(jnp.bfloat16)
-                right[index, at, length:] = (-w * spec[at, length:]).astype(jnp.bfloat16)
-        home = mxu(right[index], table_ref[...])
+                w = weights[f][c : c + 1]
+                right[index, at, :length] = (w * spec[index][at, :length]).astype(jnp.bfloat16)
+                right[index, at, length:] = (-w * spec[index][at, length:]).astype(jnp.bfloat16)
+        home.append(mxu(right[index], table_ref[...]))
+    probe = []
+    for index, members in enumerate(groups):
         values = []
-        for k, f in enumerate(at_frame):
+        for k, f in enumerate(members):
             gr = mail(f, 1, 0, BS)
             gi = mail(f, 1, BS, BS)
             for c in range(coils):
                 at = slice((k * coils + c) * BS, (k * coils + c + 1) * BS)
                 sr, si = sens_ref[c, 0], sens_ref[c, 1]
-                br, bi = home[at, :length], home[at, length:]
+                br, bi = home[index][at, :length], home[index][at, length:]
                 gr = gr + (sr * br - si * bi)
                 gi = gi - (sr * bi + si * br)
             grad_ref[f, :BS, :] = gr
@@ -450,44 +493,18 @@
             num = num + fold(gr * gr + gi * gi)
             values.append((gr, gi))
         coil_image(index, values)
-        probe = mxu(left[index], table_ref[...])
-        for k in range(group):
+        probe.append(mxu(left[index], table_ref[...]))
+    put_kind(1, lambda f, g: est_ref[f] * grad_ref[g] + est_ref[g] * grad_ref[f])
+    put_kind(2, lambda f, g: grad_ref[f] * grad_ref[g])
+    for index, members in enumerate(groups):
+        for k, f in enumerate(members):
             for c in range(coils):
                 at = slice((k * coils + c) * BS, (k * coils + c + 1) * BS)
-                pr, pi = probe[at, :length], probe[at, length:]
-                den = den + weights[k][c : c + 1] * fold(pr * pr + pi * pi)
-        return num, den
-
-    for index in range(frames // group):
-        num, den = passes(index, (num, den))
+                pr, pi = probe[index][at, :length], probe[index][at, length:]
+                den = den + weights[f][c : c + 1] * fold(pr * pr + pi * pi)
     numer = jnp.sum(jnp.sum(num, axis=0, keepdims=True), axis=1, keepdims=True)
     denom = jnp.sum(jnp.sum(den, axis=0, keepdims=True), axis=1, keepdims=True)
 
-    edge = lax.rem(offsets_ref[0, 0] - offsets_ref[1, 0] + BS, BS)
-    low = [(iota((8, length), 0) + 8 * t >= edge) for t in range(BS // 8)]
-    block = len(pairs)
-    span = out_ref.shape[2]
-
-    def rows_of(product):
-        return [
-            sum(product[p * BS + 8 * t : p * BS + 8 * t + 8] for p in range(2)) for t in range(BS // 8)
-        ]
-
-    def put(part, place, tile):
-        for half in range(length // LANES):
-            terms[half, (part * span + place) * 8 : (part * span + place) * 8 + 8, :] = tile[
-                :, half * LANES : (half + 1) * LANES
-            ]
-
-    for part in range(2):
-        for place in range(3 * block, span):
-            put(part, place, jnp.zeros((8, length), jnp.float32))
-    for place, (f, g) in enumerate(pairs):
-        ef, eg, gf, gg = est_ref[f], est_ref[g], grad_ref[f], grad_ref[g]
-        for kind, product in enumerate((ef * eg, ef * gg + eg * gf, gf * gg)):
-            rows = rows_of(product)
-            put(0, kind * block + place, sum(jnp.where(low[t], rows[t], 0.0) for t in range(BS // 8)))
-            put(1, kind * block + place, sum(jnp.where(low[t], 0.0, rows[t]) for t in range(BS // 8)))
     shift = offsets_ref[1, 1]
     blocks = length // BS
     member = (block_of(iota((blocks, length), 1), shift, length) == iota((blocks, length), 0)).astype(jnp.float32)
@@ -501,7 +518,7 @@
             ],
             axis=1,
         )
-        pack = exact_dot(member, sums, (((1,), (1,)), ((), ())))
+        pack = pick_rows(member, sums)
         pack = jnp.where(lane == 3 * block, numer, jnp.where(lane == 3 * block + 1, denom, pack))
         own_ref[part * blocks : (part + 1) * blocks, :] = pack
         packs.append(pack)
@@ -531,13 +548,13 @@
     gram = total - step * cross + step * step * square
     gram = jnp.concatenate([gram, jnp.zeros((LANES - 2 * blocks, span), jnp.float32)], axis=0)
     gram = jnp.where(iota(gram.shape, 1) < block, gram, 0.0)
-    gram = exact_dot(select_ref[...], gram, (((1,), (1,)), ((), ())))
+    gram = pick_rows(select_ref[...], gram)
     factors = shrink_factors(gram, held, other, frames)
     shift = offsets_ref[1, 1]
     column = block_of(iota((LANES, length), 1), shift, length)
     row = iota((LANES, length), 0)
-    spread_low[...] = exact_dot(factors, (column == row).astype(jnp.float32))
-    spread_up[...] = exact_dot(factors, (column + blocks == row).astype(jnp.float32))
+    spread_low[...] = pick(factors, (column == row).astype(jnp.float32))
+    spread_up[...] = pick(factors, (column + blocks == row).astype(jnp.float32))
     edge = lax.rem(offsets_ref[0, 0] - offsets_ref[1, 0] + BS, BS)
     moved = [est_ref[f] - step * grad_ref[f] for f in range(frames)]
     for t in range(BS // 8):
@@ -553,13 +570,17 @@
                 out_ref[f, rows, :] = moved[f][rows] - total[p]
 
 
-def place_kernel(offsets_ref, strips_ref, out_ref):
-    strips, strip, length = strips_ref.shape
+def place_kernel(offsets_ref, strips_ref, out_hbm, whole, sems):
+    strips, _, length = strips_ref.shape
     width = strips * BS
     shift = lax.rem(width - offsets_ref[0, 0], width)
+    copies = []
     for part in range(2):
-        whole = strips_ref[:, part * BS : (part + 1) * BS, :].reshape(width, length)
-        out_ref[0, part] = pltpu.roll(whole, shift, 0)
+        whole[part] = pltpu.roll(strips_ref[:, part * BS : (part + 1) * BS, :].reshape(width, length), shift, 0)
+        copies.append(pltpu.make_async_copy(whole.at[part], out_hbm.at[0, part], sems.at[part]))
+        copies[-1].start()
+    for copy in copies:
+        copy.wait()
 
 
 def vmem():
@@ -586,24 +607,20 @@
     return pltpu.CompilerParams(vmem_limit_bytes=mebibytes * 1024 * 1024)
 
 
-def strips_body(start_image, sensitivity, kspace, sampled, offsets):
+def frame_call(start_image, sensitivity, kspace, sampled, offsets, table):
     _, _, width, length = start_image.shape
     coils = sensitivity.shape[0]
-    strips = width // BS
-    frames = strips
-    table = jnp.asarray(wide_table(length))
-    strip = 2 * BS
-    span = LANES
-    blocks = length // BS
-    halves = length // LANES
-
     rows = 2 * BS
     chunks = width // rows
-    mail = pl.pallas_call(
+    return pl.pallas_call(
         frame_kernel,
-        out_shape=f32(strips, halves * (2 * strip + coils) + 8, LANES),
+        out_shape=(
+            pltpu.VMEM((width // BS, length // LANES * (4 * BS + coils) + 8, LANES), jnp.float32),
+            pltpu.VMEM((coils, 2, BS, length), jnp.float32),
+            pltpu.VMEM(offsets.shape, jnp.int32),
+        ),
         in_specs=[hbm()] * 6,
-        out_specs=vmem(),
+        out_specs=(vmem(),) * 3,
         scratch_shapes=[
             pltpu.SMEM(offsets.shape, jnp.int32),
             pltpu.VMEM(start_image.shape, jnp.float32),
@@ -618,34 +635,28 @@
             pltpu.SemaphoreType.DMA((2, chunks)),
         ],
         compiler_params=params(60),
-        cost_estimate=pl.CostEstimate(flops=24 * coils * width * length * length, bytes_accessed=4 * 10**6, transcendentals=0),
+        name="frame_gradient",
     )(offsets, start_image, sensitivity, kspace, sampled, table)
-    mail = exchange(mail)
-
-    sens = pl.pallas_call(
-        strip_kernel,
-        out_shape=f32(coils, 2, BS, length),
-        in_specs=[smem(), hbm()],
-        out_specs=vmem(),
-        scratch_shapes=[pltpu.VMEM((2, coils, 2, BS, length), jnp.bfloat16), pltpu.SemaphoreType.DMA((2,))],
-        compiler_params=params(),
-        cost_estimate=pl.CostEstimate(flops=10**6, bytes_accessed=10**6, transcendentals=0),
-    )(offsets, sensitivity)
-
+
+
+def middle_call(mail, sens, offsets, table):
+    frames = mail.shape[0]
+    coils, _, _, length = sens.shape
     count = frames * frames
+    blocks = length // BS
     group = 2
-    sent, own, estimate, gradient = pl.pallas_call(
+    return pl.pallas_call(
         middle_kernel,
         out_shape=(
-            f32(strips, blocks, span),
-            f32(2 * blocks, span),
-            f32(frames, strip, length),
-            f32(frames, strip, length),
+            f32(frames, blocks, LANES),
+            f32(2 * blocks, LANES),
+            f32(frames, 2 * BS, length),
+            f32(frames, 2 * BS, length),
         ),
         in_specs=[smem()] + [vmem()] * 3,
         out_specs=(vmem(),) * 4,
         scratch_shapes=[
-            pltpu.VMEM((length // LANES, 2 * span * 8, LANES), jnp.float32),
+            pltpu.VMEM((length // LANES, 2 * LANES * 8, LANES), jnp.float32),
             pltpu.VMEM((count, LANES), jnp.float32),
             pltpu.VMEM((count, LANES), jnp.float32),
             pltpu.VMEM((count, length), jnp.float32),
@@ -653,11 +664,14 @@
             pltpu.VMEM((frames // group, group * coils * BS, 2 * length), jnp.bfloat16),
         ],
         compiler_params=params(),
-        cost_estimate=pl.CostEstimate(flops=24 * coils * width * length * length, bytes_accessed=4 * 10**6, transcendentals=0),
+        name="strip_shrink_gradient",
     )(offsets, mail, sens, table)
-    heard = exchange(sent)
-
-    returned = pl.pallas_call(
+
+
+def last_call(own, heard, estimate, gradient, offsets):
+    frames, strip, length = estimate.shape
+    count = frames * frames
+    return pl.pallas_call(
         last_kernel,
         out_shape=f32(frames, strip, length),
         in_specs=[smem()] + [vmem()] * 5,
@@ -669,16 +683,31 @@
             pltpu.VMEM((count, length), jnp.float32),
         ],
         compiler_params=params(),
-    )(offsets, own, heard, estimate, gradient, jnp.asarray(pair_select(frames, span)))
-    returned = exchange(returned)
-
+        name="strip_shrink",
+    )(offsets, own, heard, estimate, gradient, jnp.asarray(pair_select(frames, LANES)))
+
+
+def place_call(strips, offsets):
+    count, strip, length = strips.shape
+    width = count * strip // 2
     return pl.pallas_call(
         place_kernel,
         out_shape=f32(1, 2, width, length),
         in_specs=[smem(), vmem()],
-        out_specs=vmem(),
+        out_specs=hbm(),
+        scratch_shapes=[pltpu.VMEM((2, width, length), jnp.float32), pltpu.SemaphoreType.DMA((2,))],
         compiler_params=params(),
-    )(offsets, returned)
+        name="frame_place",
+    )(offsets, strips)
+
+
+def strips_body(start_image, sensitivity, kspace, sampled, offsets):
+    table = jnp.asarray(wide_table(start_image.shape[3]))
+    mail, sens, offsets = frame_call(start_image, sensitivity, kspace, sampled, offsets, table)
+    mail = exchange(mail)
+    sent, own, estimate, gradient = middle_call(mail, sens, offsets, table)
+    returned = exchange(last_call(own, exchange(sent), estimate, gradient, offsets))
+    return place_call(returned, offsets)
 
 
 def fits_strips(start_image, sensitivity, kspace, sampled, offsets):

time: 59.8 us -> 57.4 us (0.960)
  blocking collectives: 21.1 us -> 44.7 us
  waiting for transfers between devices: 15.9 us -> 0 us
  starting transfers between devices: 7.39 us -> 0 us
  Pallas kernels: 14.9 us -> 12.3 us
    all_to_all x2 -> x3, blocking collectives: 21.1 us -> 44.7 us  [exchange(): return lax.all_to_all(blocks, 'tm', split_axis=0, concat_axis=0, tiled=True)]
    all_to_all x1 -> x0, waiting for transfers between devices: 15.9 us -> none  [exchange(): return lax.all_to_all(blocks, 'tm', split_axis=0, concat_axis=0, tiled=True)]
    all_to_all x1 -> x0, starting transfers between devices: 7.39 us -> none  [exchange(): return lax.all_to_all(blocks, 'tm', split_axis=0, concat_axis=0, tiled=True)]
    pallas_call x5 -> x4, Pallas kernels: 14.9 us -> 12.3 us  [the longest x1 5.39 us: frame_call(): pl.pallas_call(frame_kernel, out_shape=(pltpu.VMEM((width // BS, length /...]
  transfers between devices with their start and end apart: 1 -> 0, of which waited for: 1 -> 0; matrix products, arithmetic and copies ran while one was open for 0% -> 0% of each run, Pallas kernels for 1% -> 0%
where the time goes in v2:
time: 57.4 us; the launch traced here: 57.1 us
  blocking collectives  44.7 us (78%)
  Pallas kernels  12.3 us (21%)
    all_to_all x3, blocking collectives, exchange(): return lax.all_to_all(blocks, 'tm', split_axis=0, concat_axis=0, tiled=True)  44.7 us
    pallas_call x1, Pallas kernels, frame_call(): pl.pallas_call(frame_kernel, out_shape=(pltpu.VMEM((width // BS, length /...  5.39 us
    pallas_call x1, Pallas kernels, middle_call(): pl.pallas_call(middle_kernel, out_shape=(f32(frames, blocks, LANES), f32(...  4.15 us
    pallas_call x1, Pallas kernels, last_call(): pl.pallas_call(last_kernel, out_shape=f32(frames, strip, length), in_spec...  1.44 us
    pallas_call x1, Pallas kernels, place_call(): pl.pallas_call(place_kernel, out_shape=f32(1, 2, width, length), in_specs...  1.3 us

profile of v2, /device:TPU:0, one launch (start us, length us, event | category | flops | bytes accessed | tf_op | source)
XLA Modules:
  0.0 57.1 jit_solution(16476702479655664621)
XLA Ops:
  0.0 5.4 %frame_gradient.1 = (f32[8,152,128]{2,1,0:T(8,128)S(1)}, f32[8,2,16,256]{3,2,1,0:T(8,128)S(1)}, s32[2,2]{1,0:T(2,128)S(1)}) custom-call(s32[2,2]{1,0:T(2,128)} %offsets_hbm.1, f32[1,2,128,256]{3,2,1,0:T(8,128)} %start_hbm.1, bf16[8,2,128,256]{3,2,1,0:T(8,128)(2,1)} %sens_hbm.1, bf16[1,8,2,128,256]{4,3,2,1,0:T(8,128)(2,1)} %data_hbm.1, ...), custom_call_target="tpu_custom_call" | custom-call | tf_op jit(solution)/shard_map/frame_gradient/pallas_call | solution.py:615
  5.4 0.0 copy-start
  5.4 24.3 %all_to_all.15.mail_ref = f32[8,152,128]{2,1,0:T(8,128)S(1)} all-to-all(f32[8,152,128]{2,1,0:T(8,128)S(1)} %get-tuple-element.13), channel_id=1, replica_groups=mesh['tm'=8,'cuts'=4] {'tm'}, dimensions={0} | all-to-all | bytes 1245184 | tf_op jit(solution)/shard_map/all_to_all | solution.py:603
  29.7 0.0 copy-done
  29.7 4.2 %strip_shrink_gradient.1 = (f32[8,16,128]{2,1,0:T(8,128)S(1)}, f32[32,128]{1,0:T(8,128)S(1)}, f32[8,32,256]{2,1,0:T(8,128)S(1)}, f32[8,32,256]{2,1,0:T(8,128)S(1)}) custom-call(s32[2,2]{1,0:T(2,128)S(1)} %get-tuple-element.12.offsets_ref, f32[8,152,128]{2,1,0:T(8,128)S(1)} %all_to_all.15.mail_ref, f32[8,2,16,256]{3,2,1,0:T(8,128)S(1)} %get-tuple-element.14.sens_ref, ...), custom_call_target="tpu_custom_call" | custom-call | tf_op jit(solution)/shard_map/strip_shrink_gradient/pallas_call | solution.py:648
  33.9 0.0 copy-start.1
  33.9 9.8 %all_to_all.16.heard_ref = f32[8,16,128]{2,1,0:T(8,128)S(1)} all-to-all(f32[8,16,128]{2,1,0:T(8,128)S(1)} %get-tuple-element.16), channel_id=1, replica_groups=mesh['tm'=8,'cuts'=4] {'tm'}, dimensions={0} | all-to-all | bytes 131072 | tf_op jit(solution)/shard_map/all_to_all | solution.py:603
  43.7 0.0 copy-done.1
  43.7 1.4 %strip_shrink.1 = f32[8,32,256]{2,1,0:T(8,128)S(1)} custom-call(s32[2,2]{1,0:T(2,128)S(1)} %get-tuple-element.12.offsets_ref, f32[32,128]{1,0:T(8,128)S(1)} %get-tuple-element.15.own_ref, f32[8,16,128]{2,1,0:T(8,128)S(1)} %all_to_all.16.heard_ref, f32[8,32,256]{2,1,0:T(8,128)S(1)} %get-tuple-element.17.est_ref, ...), custom_call_target="tpu_custom_call" | custom-call | tf_op jit(solution)/shard_map/strip_shrink/pallas_call | solution.py:674
  45.1 10.6 %all_to_all.17.strips_ref = f32[8,32,256]{2,1,0:T(8,128)S(1)} all-to-all(f32[8,32,256]{2,1,0:T(8,128)S(1)} %strip_shrink.1), channel_id=1, replica_groups=mesh['tm'=8,'cuts'=4] {'tm'}, dimensions={0} | all-to-all | bytes 524288 | tf_op jit(solution)/shard_map/all_to_all | solution.py:603
  55.8 1.3 %frame_place.1 = f32[1,2,128,256]{3,2,1,0:T(8,128)} custom-call(s32[2,2]{1,0:T(2,128)S(1)} %get-tuple-element.12.offsets_ref, f32[8,32,256]{2,1,0:T(8,128)S(1)} %all_to_all.17.strips_ref), custom_call_target="tpu_custom_call" | custom-call | tf_op jit(solution)/shard_map/frame_place/pallas_call | solution.py:693
Async XLA Ops:
  5.4 24.3 %copy-start = (bf16[512,512]{1,0:T(8,128)(2,1)S(1)}, bf16[512,512]{1,0:T(8,128)(2,1)}, u32[]{:S(2)}) copy-start(bf16[512,512]{1,0:T(8,128)(2,1)} %constant.4.clone.table_hbm.table_ref) | copy-start | bytes 1572868
  33.9 9.8 %copy-start.1 = (f32[64,128]{1,0:T(8,128)S(1)}, f32[64,128]{1,0:T(8,128)}, u32[]{:S(2)}) copy-start(f32[64,128]{1,0:T(8,128)} %constant.5.clone.select_ref) | copy-start | bytes 98308

commit v3 on v2

--- a/solution.py
+++ b/solution.py
@@ -147,12 +147,24 @@
     return estimate
 
 
-def block_of(column, shift, length):
-    return lax.rem(column + shift, length) // BS
-
-
 def iota(shape, dim):
     return lax.broadcasted_iota(jnp.int32, shape, dim)
+
+
+def in_block(column, shift, block, length):
+    moved = column + shift
+    moved = jnp.where(moved >= length, moved - length, moved)
+    return (moved >= block * BS) & (moved < block * BS + BS)
+
+
+def offset_row(offsets_ref, iteration, axis, lanes):
+    at = 2 * iteration + axis
+    return jnp.concatenate([offsets_ref[at : at + 1, :]] * (lanes // LANES), axis=1)
+
+
+def upper_rows(offsets_ref, length):
+    edge = offset_row(offsets_ref, 0, 0, length) - offset_row(offsets_ref, 1, 0, length)
+    return jnp.where(edge < 0, edge + BS, edge)
 
 
 def wide_table(length):
@@ -187,14 +199,14 @@
 
 def pick(x, ones):
     rows = x.shape[0]
-    out = mxu(pieces(x), ones.astype(jnp.bfloat16))
+    out = mxu(pieces(x), ones.astype(jnp.float32).astype(jnp.bfloat16))
     return out[:rows] + out[rows : 2 * rows] + out[2 * rows :]
 
 
 def pick_rows(ones, x):
     rows = x.shape[0]
     out = lax.dot_general(
-        ones.astype(jnp.bfloat16), pieces(x), (((1,), (1,)), ((), ())), preferred_element_type=jnp.float32
+        ones.astype(jnp.float32).astype(jnp.bfloat16), pieces(x), (((1,), (1,)), ((), ())), preferred_element_type=jnp.float32
     )
     return out[:, :rows] + out[:, rows : 2 * rows] + out[:, 2 * rows :]
 
@@ -258,10 +270,9 @@
     start_copy.wait()
     lines_copy.wait()
     copied = jnp.zeros(copied_ref.shape, jnp.int32)
-    for k in range(copied.shape[0]):
-        for axis in range(copied.shape[1]):
-            here = (iota(copied.shape, 0) == k) & (iota(copied.shape, 1) == axis)
-            copied = jnp.where(here, offsets_ref[k, axis], copied)
+    for k in range(ITERS):
+        for axis in range(2):
+            copied = jnp.where(iota(copied.shape, 0) == 2 * k + axis, offsets_ref[k, axis], copied)
     copied_ref[...] = copied
     weight = lines_ref[0].astype(jnp.float32)
     post(0, start_ref.at[0])
@@ -327,15 +338,11 @@
         out_ref[target, base : base + 8, :] = sums
 
 
-def newton_inverse(system, held, other, frames):
-    lanes = system[0].shape[1]
-    place = iota((frames, lanes), 0)
+def newton_inverse(system, held, frames):
+    place = iota(system[0].shape, 0)
     unit = [(place == f).astype(jnp.float32) for f in range(frames)]
-    sums = sum(jnp.abs(tile) for tile in system)
-    bound = jnp.max(sums, axis=0, keepdims=True)
-    for f in range(frames):
-        held[f * frames : (f + 1) * frames, :] = system[f]
-    approx = [unit[f] / bound for f in range(frames)]
+    bound = jnp.max(sum(jnp.abs(tile) for tile in system), axis=0, keepdims=True)
+    scale = 1.0 / bound
 
     def times(ref, tiles):
         out = []
@@ -346,29 +353,34 @@
             out.append(terms[0])
         return out
 
-    for newton in range(NEWTON):
+    power = [unit[f] - scale * system[f] for f in range(frames)]
+    total = [unit[f] + power[f] for f in range(frames)]
+    for newton in range(1, NEWTON):
         for f in range(frames):
-            other[f * frames : (f + 1) * frames, :] = approx[f]
-        product = times(held, approx)
-        approx = times(other, [2.0 * unit[f] - product[f] for f in range(frames)])
-    return approx
-
-
-def shrink_factors(gram, held, other, frames):
+            held[newton, f * frames : (f + 1) * frames, :] = power[f]
+        power = times(held.at[newton], power)
+        for f in range(frames):
+            held[0, f * frames : (f + 1) * frames, :] = power[f]
+        added = times(held.at[0], total)
+        total = [total[f] + added[f] for f in range(frames)]
+    return [scale * tile for tile in total]
+
+
+def shrink_factors(gram, held, frames):
     lanes = gram.shape[1]
     place = iota((frames, lanes), 0)
     tiles = [gram[f * frames : (f + 1) * frames, :] for f in range(frames)]
     trace = sum(gram[f * frames + f : f * frames + f + 1, :] for f in range(frames))
     level = shrink_ratio * trace / frames + epsilon
     system = [tiles[f] + jnp.where(place == f, level, 0.0) for f in range(frames)]
-    approx = newton_inverse(system, held, other, frames)
+    approx = newton_inverse(system, held, frames)
     return jnp.concatenate([level * tile for tile in approx], axis=0)
 
 
 def middle_kernel(
     offsets_ref, mail_ref, sens_ref, table_ref,
     out_ref, own_ref, est_ref, grad_ref,
-    terms, held, other, spread, left, right,
+    terms, held, spread, left, right,
 ):
     frames = mail_ref.shape[0]
     coils, _, _, length = sens_ref.shape
@@ -406,10 +418,9 @@
     sums = jnp.concatenate(
         [sum(terms[half, pl.ds(s, count, stride=8), :] for s in range(8)) for half in range(length // LANES)], axis=1
     )
-    shift = offsets_ref[0, 1]
-    tall = (block_of(iota((length, LANES), 0), shift, length) == iota((length, LANES), 1)).astype(jnp.float32)
-    broad = (block_of(iota((LANES, length), 1), shift, length) == iota((LANES, length), 0)).astype(jnp.float32)
-    factors = shrink_factors(pick(sums, tall), held, other, frames)
+    tall = in_block(iota((length, LANES), 0), offset_row(offsets_ref, 0, 1, LANES), iota((length, LANES), 1), length)
+    broad = in_block(iota((LANES, length), 1), offset_row(offsets_ref, 0, 1, length), iota((LANES, length), 0), length)
+    factors = shrink_factors(pick(sums, tall), held, frames)
     spread[...] = pick(factors, broad)
     moved = [est_ref[f] for f in range(frames)]
     for f in range(frames):
@@ -432,7 +443,7 @@
                 left[index, at, :length] = (sr * a - si * b).astype(jnp.bfloat16)
                 left[index, at, length:] = (sr * b + si * a).astype(jnp.bfloat16)
 
-    edge = lax.rem(offsets_ref[0, 0] - offsets_ref[1, 0] + BS, BS)
+    edge = upper_rows(offsets_ref, length)
     low = [(iota((8, length), 0) + 8 * t >= edge) for t in range(BS // 8)]
     block = len(pairs)
     span = out_ref.shape[2]
@@ -505,9 +516,9 @@
     numer = jnp.sum(jnp.sum(num, axis=0, keepdims=True), axis=1, keepdims=True)
     denom = jnp.sum(jnp.sum(den, axis=0, keepdims=True), axis=1, keepdims=True)
 
-    shift = offsets_ref[1, 1]
     blocks = length // BS
-    member = (block_of(iota((blocks, length), 1), shift, length) == iota((blocks, length), 0)).astype(jnp.float32)
+    shift = offset_row(offsets_ref, 1, 1, length)
+    member = in_block(iota((blocks, length), 1), shift, iota((blocks, length), 0), length)
     lane = iota((blocks, span), 1)
     packs = []
     for part in range(2):
@@ -529,7 +540,7 @@
         out_ref[target] = jnp.where(before == target, packs[1], packs[0])
 
 
-def last_kernel(offsets_ref, own_ref, heard_ref, est_ref, grad_ref, select_ref, out_ref, held, other, spread_low, spread_up):
+def last_kernel(offsets_ref, own_ref, heard_ref, est_ref, grad_ref, select_ref, out_ref, held, spread):
     frames, strip, length = est_ref.shape
     strips, blocks, span = heard_ref.shape
     block = len(pair_list(frames))
@@ -549,13 +560,13 @@
     gram = jnp.concatenate([gram, jnp.zeros((LANES - 2 * blocks, span), jnp.float32)], axis=0)
     gram = jnp.where(iota(gram.shape, 1) < block, gram, 0.0)
     gram = pick_rows(select_ref[...], gram)
-    factors = shrink_factors(gram, held, other, frames)
-    shift = offsets_ref[1, 1]
-    column = block_of(iota((LANES, length), 1), shift, length)
+    factors = shrink_factors(gram, held, frames)
+    shift = offset_row(offsets_ref, 1, 1, length)
+    column = iota((LANES, length), 1)
     row = iota((LANES, length), 0)
-    spread_low[...] = pick(factors, (column == row).astype(jnp.float32))
-    spread_up[...] = pick(factors, (column + blocks == row).astype(jnp.float32))
-    edge = lax.rem(offsets_ref[0, 0] - offsets_ref[1, 0] + BS, BS)
+    broad = [in_block(column, shift, row - part * blocks, length).astype(jnp.float32) for part in range(2)]
+    spread[...] = pick(factors, jnp.concatenate(broad, axis=1))
+    edge = upper_rows(offsets_ref, length)
     moved = [est_ref[f] - step * grad_ref[f] for f in range(frames)]
     for t in range(BS // 8):
         low = iota((8, length), 0) + 8 * t >= edge
@@ -563,7 +574,7 @@
             total = [jnp.zeros((8, length), jnp.float32)] * 2
             for g in range(frames):
                 at = f * frames + g
-                factor = jnp.where(low, spread_low[at : at + 1, :], spread_up[at : at + 1, :])
+                factor = jnp.where(low, spread[at : at + 1, :length], spread[at : at + 1, length:])
                 total = [total[p] + factor * moved[g][p * BS + 8 * t : p * BS + 8 * t + 8] for p in range(2)]
             for p in range(2):
                 rows = slice(p * BS + 8 * t, p * BS + 8 * t + 8)
@@ -573,10 +584,15 @@
 def place_kernel(offsets_ref, strips_ref, out_hbm, whole, sems):
     strips, _, length = strips_ref.shape
     width = strips * BS
-    shift = lax.rem(width - offsets_ref[0, 0], width)
+    shift = offset_row(offsets_ref, 0, 0, length)
     copies = []
     for part in range(2):
-        whole[part] = pltpu.roll(strips_ref[:, part * BS : (part + 1) * BS, :].reshape(width, length), shift, 0)
+        image = strips_ref[:, part * BS : (part + 1) * BS, :].reshape(width, length)
+        step = 1
+        while step < BS:
+            image = jnp.where((shift & step) != 0, pltpu.roll(image, width - step, 0), image)
+            step *= 2
+        whole[part] = image
         copies.append(pltpu.make_async_copy(whole.at[part], out_hbm.at[0, part], sems.at[part]))
         copies[-1].start()
     for copy in copies:
@@ -591,10 +607,6 @@
     return pl.BlockSpec(memory_space=pltpu.HBM)
 
 
-def smem():
-    return pl.BlockSpec(memory_space=pltpu.SMEM)
-
-
 def f32(*shape):
     return jax.ShapeDtypeStruct(shape, jnp.float32)
 
@@ -610,14 +622,14 @@
 def frame_call(start_image, sensitivity, kspace, sampled, offsets, table):
     _, _, width, length = start_image.shape
     coils = sensitivity.shape[0]
-    rows = 2 * BS
+    rows = 4 * BS
     chunks = width // rows
     return pl.pallas_call(
         frame_kernel,
         out_shape=(
             pltpu.VMEM((width // BS, length // LANES * (4 * BS + coils) + 8, LANES), jnp.float32),
             pltpu.VMEM((coils, 2, BS, length), jnp.float32),
-            pltpu.VMEM(offsets.shape, jnp.int32),
+            pltpu.VMEM((SUBLANES, LANES), jnp.int32),
         ),
         in_specs=[hbm()] * 6,
         out_specs=(vmem(),) * 3,
@@ -644,7 +656,7 @@
     coils, _, _, length = sens.shape
     count = frames * frames
     blocks = length // BS
-    group = 2
+    group = 4
     return pl.pallas_call(
         middle_kernel,
         out_shape=(
@@ -653,12 +665,11 @@
             f32(frames, 2 * BS, length),
             f32(frames, 2 * BS, length),
         ),
-        in_specs=[smem()] + [vmem()] * 3,
+        in_specs=[vmem()] * 4,
         out_specs=(vmem(),) * 4,
         scratch_shapes=[
             pltpu.VMEM((length // LANES, 2 * LANES * 8, LANES), jnp.float32),
-            pltpu.VMEM((count, LANES), jnp.float32),
-            pltpu.VMEM((count, LANES), jnp.float32),
+            pltpu.VMEM((NEWTON, count, LANES), jnp.float32),
             pltpu.VMEM((count, length), jnp.float32),
             pltpu.VMEM((frames // group, group * coils * BS, 2 * length), jnp.bfloat16),
             pltpu.VMEM((frames // group, group * coils * BS, 2 * length), jnp.bfloat16),
@@ -674,13 +685,11 @@
     return pl.pallas_call(
         last_kernel,
         out_shape=f32(frames, strip, length),
-        in_specs=[smem()] + [vmem()] * 5,
+        in_specs=[vmem()] * 6,
         out_specs=vmem(),
         scratch_shapes=[
-            pltpu.VMEM((count, LANES), jnp.float32),
-            pltpu.VMEM((count, LANES), jnp.float32),
-            pltpu.VMEM((count, length), jnp.float32),
-            pltpu.VMEM((count, length), jnp.float32),
+            pltpu.VMEM((NEWTON, count, LANES), jnp.float32),
+            pltpu.VMEM((count, 2 * length), jnp.float32),
         ],
         compiler_params=params(),
         name="strip_shrink",
@@ -693,7 +702,7 @@
     return pl.pallas_call(
         place_kernel,
         out_shape=f32(1, 2, width, length),
-        in_specs=[smem(), vmem()],
+        in_specs=[vmem()] * 2,
         out_specs=hbm(),
         scratch_shapes=[pltpu.VMEM((2, width, length), jnp.float32), pltpu.SemaphoreType.DMA((2,))],
         compiler_params=params(),

time: 57.4 us -> 54.7 us (0.953)
  Pallas kernels: 12.3 us -> 9.59 us
    pallas_call x1, Pallas kernels: 5.39 us -> 4.54 us  [frame_call(): pl.pallas_call(frame_kernel, out_shape=(pltpu.VMEM((width // BS, length /...]
    pallas_call x1, Pallas kernels: 4.15 us -> 3.4 us  [middle_call(): pl.pallas_call(middle_kernel, out_shape=(f32(frames, blocks, LANES), f32(...]
where the time goes in v3:
time: 54.7 us; the launch traced here: 54.4 us
  blocking collectives  44.7 us (82%)
  Pallas kernels  9.59 us (18%)
    all_to_all x3, blocking collectives, exchange(): return lax.all_to_all(blocks, 'tm', split_axis=0, concat_axis=0, tiled=True)  44.7 us
    pallas_call x1, Pallas kernels, frame_call(): pl.pallas_call(frame_kernel, out_shape=(pltpu.VMEM((width // BS, length /...  4.54 us
    pallas_call x1, Pallas kernels, middle_call(): pl.pallas_call(middle_kernel, out_shape=(f32(frames, blocks, LANES), f32(...  3.4 us

profile of v3, /device:TPU:0, one launch (start us, length us, event | category | flops | bytes accessed | tf_op | source)
XLA Modules:
  0.0 54.4 jit_solution(461530178620241124)
XLA Ops:
  0.0 4.5 %frame_gradient.1 = (f32[8,152,128]{2,1,0:T(8,128)S(1)}, f32[8,2,16,256]{3,2,1,0:T(8,128)S(1)}, s32[8,128]{1,0:T(8,128)S(1)}) custom-call(s32[2,2]{1,0:T(2,128)} %offsets_hbm.1, f32[1,2,128,256]{3,2,1,0:T(8,128)} %start_hbm.1, bf16[8,2,128,256]{3,2,1,0:T(8,128)(2,1)} %sens_hbm.1, bf16[1,8,2,128,256]{4,3,2,1,0:T(8,128)(2,1)} %data_hbm.1, ...), custom_call_target="tpu_custom_call" | custom-call | tf_op jit(solution)/shard_map/frame_gradient/pallas_call | solution.py:627
  4.5 0.0 copy-start
  4.6 24.3 %all_to_all.15.mail_ref = f32[8,152,128]{2,1,0:T(8,128)S(1)} all-to-all(f32[8,152,128]{2,1,0:T(8,128)S(1)} %get-tuple-element.13), channel_id=1, replica_groups=mesh['tm'=8,'cuts'=4] {'tm'}, dimensions={0} | all-to-all | bytes 1245184 | tf_op jit(solution)/shard_map/all_to_all | solution.py:615
  28.9 0.0 copy-done
  28.9 3.4 %strip_shrink_gradient.1 = (f32[8,16,128]{2,1,0:T(8,128)S(1)}, f32[32,128]{1,0:T(8,128)S(1)}, f32[8,32,256]{2,1,0:T(8,128)S(1)}, f32[8,32,256]{2,1,0:T(8,128)S(1)}) custom-call(s32[8,128]{1,0:T(8,128)S(1)} %get-tuple-element.12.offsets_ref, f32[8,152,128]{2,1,0:T(8,128)S(1)} %all_to_all.15.mail_ref, f32[8,2,16,256]{3,2,1,0:T(8,128)S(1)} %get-tuple-element.14.sens_ref, ...), custom_call_target="tpu_custom_call" | custom-call | tf_op jit(solution)/shard_map/strip_shrink_gradient/pallas_call | solution.py:660
  32.3 0.0 copy-start.1
  32.3 9.8 %all_to_all.16.heard_ref = f32[8,16,128]{2,1,0:T(8,128)S(1)} all-to-all(f32[8,16,128]{2,1,0:T(8,128)S(1)} %get-tuple-element.16), channel_id=1, replica_groups=mesh['tm'=8,'cuts'=4] {'tm'}, dimensions={0} | all-to-all | bytes 131072 | tf_op jit(solution)/shard_map/all_to_all | solution.py:615
  42.1 0.0 copy-done.1
  42.1 0.9 %strip_shrink.1 = f32[8,32,256]{2,1,0:T(8,128)S(1)} custom-call(s32[8,128]{1,0:T(8,128)S(1)} %get-tuple-element.12.offsets_ref, f32[32,128]{1,0:T(8,128)S(1)} %get-tuple-element.15.own_ref, f32[8,16,128]{2,1,0:T(8,128)S(1)} %all_to_all.16.heard_ref, f32[8,32,256]{2,1,0:T(8,128)S(1)} %get-tuple-element.17.est_ref, ...), custom_call_target="tpu_custom_call" | custom-call | tf_op jit(solution)/shard_map/strip_shrink/pallas_call | solution.py:685
  43.0 10.6 %all_to_all.17.strips_ref = f32[8,32,256]{2,1,0:T(8,128)S(1)} all-to-all(f32[8,32,256]{2,1,0:T(8,128)S(1)} %strip_shrink.1), channel_id=1, replica_groups=mesh['tm'=8,'cuts'=4] {'tm'}, dimensions={0} | all-to-all | bytes 524288 | tf_op jit(solution)/shard_map/all_to_all | solution.py:615
  53.6 0.8 %frame_place.1 = f32[1,2,128,256]{3,2,1,0:T(8,128)} custom-call(s32[8,128]{1,0:T(8,128)S(1)} %get-tuple-element.12.offsets_ref, f32[8,32,256]{2,1,0:T(8,128)S(1)} %all_to_all.17.strips_ref), custom_call_target="tpu_custom_call" | custom-call | tf_op jit(solution)/shard_map/frame_place/pallas_call | solution.py:702
Async XLA Ops:
  4.5 24.3 %copy-start = (bf16[512,512]{1,0:T(8,128)(2,1)S(1)}, bf16[512,512]{1,0:T(8,128)(2,1)}, u32[]{:S(2)}) copy-start(bf16[512,512]{1,0:T(8,128)(2,1)} %constant.4.clone.table_hbm.table_ref) | copy-start | bytes 1572868
  32.3 9.8 %copy-start.1 = (f32[64,128]{1,0:T(8,128)S(1)}, f32[64,128]{1,0:T(8,128)}, u32[]{:S(2)}) copy-start(f32[64,128]{1,0:T(8,128)} %constant.5.clone.select_ref) | copy-start | bytes 98308

commit v4 on v3

--- a/solution.py
+++ b/solution.py
@@ -283,9 +283,9 @@
     spec = []
     for i in range(chunks):
         sens_copy[i].wait()
-        coil_image(i, start_ref[0, 0, i * rows : (i + 1) * rows], start_ref[0, 1, i * rows : (i + 1) * rows])
         if i == 0:
             table_copy.wait()
+        coil_image(i, start_ref[0, 0, i * rows : (i + 1) * rows], start_ref[0, 1, i * rows : (i + 1) * rows])
         spec.append(mxu(left[i], table_ref[...]))
     me = lax.axis_index("tm")
     each = rows // BS
@@ -309,19 +309,21 @@
     num = jnp.zeros((8, length), jnp.float32)
     probe = []
     for i in range(chunks):
-        gr = jnp.zeros((rows, length), jnp.float32)
-        gi = jnp.zeros((rows, length), jnp.float32)
-        for c in range(coils):
-            sr = sens_ref[i, c, 0].astype(jnp.float32)
-            si = sens_ref[i, c, 1].astype(jnp.float32)
-            at = slice(c * rows, (c + 1) * rows)
-            br, bi = home[i][at, :length], home[i][at, length:]
-            gr = gr + (sr * br - si * bi)
-            gi = gi - (sr * bi + si * br)
-        grad[0, i * rows : (i + 1) * rows, :] = gr
-        grad[1, i * rows : (i + 1) * rows, :] = gi
-        num = num + fold(gr * gr + gi * gi)
-        coil_image(i, gr, gi)
+        for first in range(0, rows, 2 * BS):
+            some = slice(first, first + 2 * BS)
+            gr = jnp.zeros((2 * BS, length), jnp.float32)
+            gi = jnp.zeros((2 * BS, length), jnp.float32)
+            for c in range(coils):
+                sr = sens_ref[i, c, 0, some].astype(jnp.float32)
+                si = sens_ref[i, c, 1, some].astype(jnp.float32)
+                at = slice(c * rows + first, c * rows + first + 2 * BS)
+                br, bi = home[i][at, :length], home[i][at, length:]
+                gr = gr + (sr * br - si * bi)
+                gi = gi - (sr * bi + si * br)
+            grad[0, i * rows + first : i * rows + first + 2 * BS, :] = gr
+            grad[1, i * rows + first : i * rows + first + 2 * BS, :] = gi
+            num = num + fold(gr * gr + gi * gi)
+        coil_image(i, grad[0, i * rows : (i + 1) * rows], grad[1, i * rows : (i + 1) * rows])
         probe.append(mxu(left[i], table_ref[...]))
     post(1, grad)
     den = jnp.zeros((8, length), jnp.float32)
@@ -622,7 +624,7 @@
 def frame_call(start_image, sensitivity, kspace, sampled, offsets, table):
     _, _, width, length = start_image.shape
     coils = sensitivity.shape[0]
-    rows = 4 * BS
+    rows = width
     chunks = width // rows
     return pl.pallas_call(
         frame_kernel,
@@ -656,7 +658,7 @@
     coils, _, _, length = sens.shape
     count = frames * frames
     blocks = length // BS
-    group = 4
+    group = frames
     return pl.pallas_call(
         middle_kernel,
         out_shape=(

time: 54.7 us -> 54.1 us (0.989)
  Pallas kernels: 9.59 us -> 8.98 us
where the time goes in v4:
time: 54.1 us; the launch traced here: 53.8 us
  blocking collectives  44.7 us (83%)
  Pallas kernels  8.98 us (17%)
    all_to_all x3, blocking collectives, exchange(): return lax.all_to_all(blocks, 'tm', split_axis=0, concat_axis=0, tiled=True)  44.7 us
    pallas_call x1, Pallas kernels, frame_call(): pl.pallas_call(frame_kernel, out_shape=(pltpu.VMEM((width // BS, length /...  4 us
    pallas_call x1, Pallas kernels, middle_call(): pl.pallas_call(middle_kernel, out_shape=(f32(frames, blocks, LANES), f32(...  3.33 us

profile of v4, /device:TPU:0, one launch (start us, length us, event | category | flops | bytes accessed | tf_op | source)
XLA Modules:
  0.0 53.8 jit_solution(7606278092501384371)
XLA Ops:
  0.0 4.0 %frame_gradient.1 = (f32[8,152,128]{2,1,0:T(8,128)S(1)}, f32[8,2,16,256]{3,2,1,0:T(8,128)S(1)}, s32[8,128]{1,0:T(8,128)S(1)}) custom-call(s32[2,2]{1,0:T(2,128)} %offsets_hbm.1, f32[1,2,128,256]{3,2,1,0:T(8,128)} %start_hbm.1, bf16[8,2,128,256]{3,2,1,0:T(8,128)(2,1)} %sens_hbm.1, bf16[1,8,2,128,256]{4,3,2,1,0:T(8,128)(2,1)} %data_hbm.1, ...), custom_call_target="tpu_custom_call" | custom-call | tf_op jit(solution)/shard_map/frame_gradient/pallas_call | solution.py:629
  4.0 0.0 copy-start
  4.0 24.3 %all_to_all.15.mail_ref = f32[8,152,128]{2,1,0:T(8,128)S(1)} all-to-all(f32[8,152,128]{2,1,0:T(8,128)S(1)} %get-tuple-element.13), channel_id=1, replica_groups=mesh['tm'=8,'cuts'=4] {'tm'}, dimensions={0} | all-to-all | bytes 1245184 | tf_op jit(solution)/shard_map/all_to_all | solution.py:617
  28.3 0.0 copy-done
  28.3 3.3 %strip_shrink_gradient.1 = (f32[8,16,128]{2,1,0:T(8,128)S(1)}, f32[32,128]{1,0:T(8,128)S(1)}, f32[8,32,256]{2,1,0:T(8,128)S(1)}, f32[8,32,256]{2,1,0:T(8,128)S(1)}) custom-call(s32[8,128]{1,0:T(8,128)S(1)} %get-tuple-element.12.offsets_ref, f32[8,152,128]{2,1,0:T(8,128)S(1)} %all_to_all.15.mail_ref, f32[8,2,16,256]{3,2,1,0:T(8,128)S(1)} %get-tuple-element.14.sens_ref, ...), custom_call_target="tpu_custom_call" | custom-call | tf_op jit(solution)/shard_map/strip_shrink_gradient/pallas_call | solution.py:662
  31.7 0.0 copy-start.1
  31.7 9.8 %all_to_all.16.heard_ref = f32[8,16,128]{2,1,0:T(8,128)S(1)} all-to-all(f32[8,16,128]{2,1,0:T(8,128)S(1)} %get-tuple-element.16), channel_id=1, replica_groups=mesh['tm'=8,'cuts'=4] {'tm'}, dimensions={0} | all-to-all | bytes 131072 | tf_op jit(solution)/shard_map/all_to_all | solution.py:617
  41.5 0.0 copy-done.1
  41.5 0.9 %strip_shrink.1 = f32[8,32,256]{2,1,0:T(8,128)S(1)} custom-call(s32[8,128]{1,0:T(8,128)S(1)} %get-tuple-element.12.offsets_ref, f32[32,128]{1,0:T(8,128)S(1)} %get-tuple-element.15.own_ref, f32[8,16,128]{2,1,0:T(8,128)S(1)} %all_to_all.16.heard_ref, f32[8,32,256]{2,1,0:T(8,128)S(1)} %get-tuple-element.17.est_ref, ...), custom_call_target="tpu_custom_call" | custom-call | tf_op jit(solution)/shard_map/strip_shrink/pallas_call | solution.py:687
  42.4 10.6 %all_to_all.17.strips_ref = f32[8,32,256]{2,1,0:T(8,128)S(1)} all-to-all(f32[8,32,256]{2,1,0:T(8,128)S(1)} %strip_shrink.1), channel_id=1, replica_groups=mesh['tm'=8,'cuts'=4] {'tm'}, dimensions={0} | all-to-all | bytes 524288 | tf_op jit(solution)/shard_map/all_to_all | solution.py:617
  53.0 0.8 %frame_place.1 = f32[1,2,128,256]{3,2,1,0:T(8,128)} custom-call(s32[8,128]{1,0:T(8,128)S(1)} %get-tuple-element.12.offsets_ref, f32[8,32,256]{2,1,0:T(8,128)S(1)} %all_to_all.17.strips_ref), custom_call_target="tpu_custom_call" | custom-call | tf_op jit(solution)/shard_map/frame_place/pallas_call | solution.py:704
Async XLA Ops:
  4.0 24.3 %copy-start = (bf16[512,512]{1,0:T(8,128)(2,1)S(1)}, bf16[512,512]{1,0:T(8,128)(2,1)}, u32[]{:S(2)}) copy-start(bf16[512,512]{1,0:T(8,128)(2,1)} %constant.4.clone.table_hbm.table_ref) | copy-start | bytes 1572868
  31.7 9.8 %copy-start.1 = (f32[64,128]{1,0:T(8,128)S(1)}, f32[64,128]{1,0:T(8,128)}, u32[]{:S(2)}) copy-start(f32[64,128]{1,0:T(8,128)} %constant.5.clone.select_ref) | copy-start | bytes 98308

commit v5 on v4

--- a/solution.py
+++ b/solution.py
@@ -225,10 +225,16 @@
     offsets_ref, start_ref, sens_ref, data_ref, lines_ref, table_ref, grad, left, right, sems, chunk_sems,
 ):
     chunks, coils, _, rows, length = sens_ref.shape
-    start_copy, lines_copy, table_copy, offsets_copy = (
+    start_copy, lines_copy, table_copy, offsets_copy, again_copy = (
         pltpu.make_async_copy(source, target, sems.at[k])
         for k, (source, target) in enumerate(
-            ((start_hbm, start_ref), (lines_hbm, lines_ref), (table_hbm, table_ref), (offsets_hbm, offsets_ref))
+            (
+                (start_hbm, start_ref),
+                (lines_hbm, lines_ref),
+                (table_hbm, table_ref.at[: 2 * length]),
+                (offsets_hbm, offsets_ref),
+                (table_hbm, table_ref.at[2 * length :]),
+            )
         )
     )
     sens_copy = [
@@ -244,7 +250,7 @@
     lines_copy.start()
     sens_copy[0].start()
     table_copy.start()
-    for copy in sens_copy[1:] + data_copy:
+    for copy in sens_copy[1:] + data_copy + [again_copy]:
         copy.start()
     strips = out_ref.shape[0]
     halves = length // LANES
@@ -286,7 +292,7 @@
         if i == 0:
             table_copy.wait()
         coil_image(i, start_ref[0, 0, i * rows : (i + 1) * rows], start_ref[0, 1, i * rows : (i + 1) * rows])
-        spec.append(mxu(left[i], table_ref[...]))
+        spec.append(mxu(left[i], table_ref[: 2 * length]))
     me = lax.axis_index("tm")
     each = rows // BS
     pair = []
@@ -300,11 +306,19 @@
     home = []
     for i in range(chunks):
         data_copy[i].wait()
+        if i == 0:
+            again_copy.wait()
         for c in range(coils):
             at = slice(c * rows, (c + 1) * rows)
             w = weight[c : c + 1]
-            right[i, at, :length] = (w * (spec[i][at, :length] - data_ref[i, c, 0].astype(jnp.float32))).astype(jnp.bfloat16)
-            right[i, at, length:] = (w * (data_ref[i, c, 1].astype(jnp.float32) - spec[i][at, length:])).astype(jnp.bfloat16)
+            parts = (
+                w * (spec[i][at, :length] - data_ref[i, c, 0].astype(jnp.float32)),
+                w * (data_ref[i, c, 1].astype(jnp.float32) - spec[i][at, length:]),
+            )
+            for k, value in enumerate(parts):
+                main = value.astype(jnp.bfloat16)
+                right[i, at, k * length : (k + 1) * length] = main
+                right[i, at, (k + 2) * length : (k + 3) * length] = (value - main.astype(jnp.float32)).astype(jnp.bfloat16)
         home.append(mxu(right[i], table_ref[...]))
     num = jnp.zeros((8, length), jnp.float32)
     probe = []
@@ -324,7 +338,7 @@
             grad[1, i * rows + first : i * rows + first + 2 * BS, :] = gi
             num = num + fold(gr * gr + gi * gi)
         coil_image(i, grad[0, i * rows : (i + 1) * rows], grad[1, i * rows : (i + 1) * rows])
-        probe.append(mxu(left[i], table_ref[...]))
+        probe.append(mxu(left[i], table_ref[: 2 * length]))
     post(1, grad)
     den = jnp.zeros((8, length), jnp.float32)
     for i in range(chunks):
@@ -641,11 +655,11 @@
             pltpu.VMEM((chunks, coils, 2, rows, length), jnp.bfloat16),
             pltpu.VMEM((chunks, coils, 2, rows, length), jnp.bfloat16),
             pltpu.VMEM(sampled.shape, jnp.int32),
-            pltpu.VMEM(table.shape, jnp.bfloat16),
+            pltpu.VMEM((4 * length, 2 * length), jnp.bfloat16),
             pltpu.VMEM((2, width, length), jnp.float32),
             pltpu.VMEM((chunks, coils * rows, 2 * length), jnp.bfloat16),
-            pltpu.VMEM((chunks, coils * rows, 2 * length), jnp.bfloat16),
-            pltpu.SemaphoreType.DMA((4,)),
+            pltpu.VMEM((chunks, coils * rows, 4 * length), jnp.bfloat16),
+            pltpu.SemaphoreType.DMA((5,)),
             pltpu.SemaphoreType.DMA((2, chunks)),
         ],
         compiler_params=params(60),

time: 54.1 us -> 54.6 us (level)
  Pallas kernels: 8.98 us -> 9.53 us
    pallas_call x1, Pallas kernels: 4 us -> 4.56 us  [frame_call(): pl.pallas_call(frame_kernel, out_shape=(pltpu.VMEM((width // BS, length /...]
where the time goes in v5:
time: 54.6 us; the launch traced here: 54.3 us
  blocking collectives  44.7 us (82%)
  Pallas kernels  9.53 us (17%)
    all_to_all x3, blocking collectives, exchange(): return lax.all_to_all(blocks, 'tm', split_axis=0, concat_axis=0, tiled=True)  44.7 us
    pallas_call x1, Pallas kernels, frame_call(): pl.pallas_call(frame_kernel, out_shape=(pltpu.VMEM((width // BS, length /...  4.56 us
    pallas_call x1, Pallas kernels, middle_call(): pl.pallas_call(middle_kernel, out_shape=(f32(frames, blocks, LANES), f32(...  3.33 us

profile of v5, /device:TPU:0, one launch (start us, length us, event | category | flops | bytes accessed | tf_op | source)
XLA Modules:
  0.0 54.3 jit_solution(8992554815256326334)
XLA Ops:
  0.0 4.6 %frame_gradient.1 = (f32[8,152,128]{2,1,0:T(8,128)S(1)}, f32[8,2,16,256]{3,2,1,0:T(8,128)S(1)}, s32[8,128]{1,0:T(8,128)S(1)}) custom-call(s32[2,2]{1,0:T(2,128)} %offsets_hbm.1, f32[1,2,128,256]{3,2,1,0:T(8,128)} %start_hbm.1, bf16[8,2,128,256]{3,2,1,0:T(8,128)(2,1)} %sens_hbm.1, bf16[1,8,2,128,256]{4,3,2,1,0:T(8,128)(2,1)} %data_hbm.1, ...), custom_call_target="tpu_custom_call" | custom-call | tf_op jit(solution)/shard_map/frame_gradient/pallas_call | solution.py:643
  4.6 0.0 copy-start
  4.6 24.3 %all_to_all.15.mail_ref = f32[8,152,128]{2,1,0:T(8,128)S(1)} all-to-all(f32[8,152,128]{2,1,0:T(8,128)S(1)} %get-tuple-element.13), channel_id=1, replica_groups=mesh['tm'=8,'cuts'=4] {'tm'}, dimensions={0} | all-to-all | bytes 1245184 | tf_op jit(solution)/shard_map/all_to_all | solution.py:631
  28.9 0.0 copy-done
  28.9 3.3 %strip_shrink_gradient.1 = (f32[8,16,128]{2,1,0:T(8,128)S(1)}, f32[32,128]{1,0:T(8,128)S(1)}, f32[8,32,256]{2,1,0:T(8,128)S(1)}, f32[8,32,256]{2,1,0:T(8,128)S(1)}) custom-call(s32[8,128]{1,0:T(8,128)S(1)} %get-tuple-element.12.offsets_ref, f32[8,152,128]{2,1,0:T(8,128)S(1)} %all_to_all.15.mail_ref, f32[8,2,16,256]{3,2,1,0:T(8,128)S(1)} %get-tuple-element.14.sens_ref, ...), custom_call_target="tpu_custom_call" | custom-call | tf_op jit(solution)/shard_map/strip_shrink_gradient/pallas_call | solution.py:676
  32.2 0.0 copy-start.1
  32.2 9.8 %all_to_all.16.heard_ref = f32[8,16,128]{2,1,0:T(8,128)S(1)} all-to-all(f32[8,16,128]{2,1,0:T(8,128)S(1)} %get-tuple-element.16), channel_id=1, replica_groups=mesh['tm'=8,'cuts'=4] {'tm'}, dimensions={0} | all-to-all | bytes 131072 | tf_op jit(solution)/shard_map/all_to_all | solution.py:631
  42.0 0.0 copy-done.1
  42.0 0.9 %strip_shrink.1 = f32[8,32,256]{2,1,0:T(8,128)S(1)} custom-call(s32[8,128]{1,0:T(8,128)S(1)} %get-tuple-element.12.offsets_ref, f32[32,128]{1,0:T(8,128)S(1)} %get-tuple-element.15.own_ref, f32[8,16,128]{2,1,0:T(8,128)S(1)} %all_to_all.16.heard_ref, f32[8,32,256]{2,1,0:T(8,128)S(1)} %get-tuple-element.17.est_ref, ...), custom_call_target="tpu_custom_call" | custom-call | tf_op jit(solution)/shard_map/strip_shrink/pallas_call | solution.py:701
  42.9 10.6 %all_to_all.17.strips_ref = f32[8,32,256]{2,1,0:T(8,128)S(1)} all-to-all(f32[8,32,256]{2,1,0:T(8,128)S(1)} %strip_shrink.1), channel_id=1, replica_groups=mesh['tm'=8,'cuts'=4] {'tm'}, dimensions={0} | all-to-all | bytes 524288 | tf_op jit(solution)/shard_map/all_to_all | solution.py:631
  53.6 0.8 %frame_place.1 = f32[1,2,128,256]{3,2,1,0:T(8,128)} custom-call(s32[8,128]{1,0:T(8,128)S(1)} %get-tuple-element.12.offsets_ref, f32[8,32,256]{2,1,0:T(8,128)S(1)} %all_to_all.17.strips_ref), custom_call_target="tpu_custom_call" | custom-call | tf_op jit(solution)/shard_map/frame_place/pallas_call | solution.py:718
Async XLA Ops:
  4.6 24.3 %copy-start = (bf16[512,512]{1,0:T(8,128)(2,1)S(1)}, bf16[512,512]{1,0:T(8,128)(2,1)}, u32[]{:S(2)}) copy-start(bf16[512,512]{1,0:T(8,128)(2,1)} %constant.4.clone.table_hbm.table_ref) | copy-start | bytes 1572868
  32.2 9.8 %copy-start.1 = (f32[64,128]{1,0:T(8,128)S(1)}, f32[64,128]{1,0:T(8,128)}, u32[]{:S(2)}) copy-start(f32[64,128]{1,0:T(8,128)} %constant.5.clone.select_ref) | copy-start | bytes 98308

commit v6 on v4

--- a/solution.py
+++ b/solution.py
@@ -287,16 +287,6 @@
             table_copy.wait()
         coil_image(i, start_ref[0, 0, i * rows : (i + 1) * rows], start_ref[0, 1, i * rows : (i + 1) * rows])
         spec.append(mxu(left[i], table_ref[...]))
-    me = lax.axis_index("tm")
-    each = rows // BS
-    pair = []
-    for place in (lax.rem(me + strips - 1, strips), me):
-        pair.append((place // each, pl.ds(pl.multiple_of(lax.rem(place, each) * BS, BS), BS)))
-    shift = offsets_ref[0, 0]
-    for c in range(coils):
-        for part in range(2):
-            two = jnp.concatenate([sens_ref[i, c, part, at, :] for i, at in pair], axis=0).astype(jnp.float32)
-            strip_ref[c, part] = pltpu.roll(two, shift, 0)[BS:]
     home = []
     for i in range(chunks):
         data_copy[i].wait()
@@ -326,6 +316,16 @@
         coil_image(i, grad[0, i * rows : (i + 1) * rows], grad[1, i * rows : (i + 1) * rows])
         probe.append(mxu(left[i], table_ref[...]))
     post(1, grad)
+    me = lax.axis_index("tm")
+    each = rows // BS
+    pair = []
+    for place in (lax.rem(me + strips - 1, strips), me):
+        pair.append((place // each, pl.ds(pl.multiple_of(lax.rem(place, each) * BS, BS), BS)))
+    shift = offsets_ref[0, 0]
+    for c in range(coils):
+        for part in range(2):
+            two = jnp.concatenate([sens_ref[i, c, part, at, :] for i, at in pair], axis=0).astype(jnp.float32)
+            strip_ref[c, part] = pltpu.roll(two, shift, 0)[BS:]
     den = jnp.zeros((8, length), jnp.float32)
     for i in range(chunks):
         for c in range(coils):
@@ -486,8 +486,8 @@
             for c in range(coils):
                 at = slice((k * coils + c) * BS, (k * coils + c + 1) * BS)
                 w = weights[f][c : c + 1]
-                right[index, at, :length] = (w * spec[index][at, :length]).astype(jnp.bfloat16)
-                right[index, at, length:] = (-w * spec[index][at, length:]).astype(jnp.bfloat16)
+                right[index, at, :length] = w.astype(jnp.bfloat16) * spec[index][at, :length].astype(jnp.bfloat16)
+                right[index, at, length:] = (-w).astype(jnp.bfloat16) * spec[index][at, length:].astype(jnp.bfloat16)
         home.append(mxu(right[index], table_ref[...]))
     probe = []
     for index, members in enumerate(groups):

time: 54.1 us -> 54.1 us (level)
  no operation moved by 1% of the time
where the time goes in v6:
time: 54.1 us; the launch traced here: 53.8 us
  blocking collectives  44.7 us (83%)
  Pallas kernels  9.01 us (17%)
    all_to_all x3, blocking collectives, exchange(): return lax.all_to_all(blocks, 'tm', split_axis=0, concat_axis=0, tiled=True)  44.7 us
    pallas_call x1, Pallas kernels, frame_call(): pl.pallas_call(frame_kernel, out_shape=(pltpu.VMEM((width // BS, length /...  4.02 us
    pallas_call x1, Pallas kernels, middle_call(): pl.pallas_call(middle_kernel, out_shape=(f32(frames, blocks, LANES), f32(...  3.35 us

profile of v6, /device:TPU:0, one launch (start us, length us, event | category | flops | bytes accessed | tf_op | source)
XLA Modules:
  0.0 53.8 jit_solution(17900666158670154419)
XLA Ops:
  0.0 4.0 %frame_gradient.1 = (f32[8,152,128]{2,1,0:T(8,128)S(1)}, f32[8,2,16,256]{3,2,1,0:T(8,128)S(1)}, s32[8,128]{1,0:T(8,128)S(1)}) custom-call(s32[2,2]{1,0:T(2,128)} %offsets_hbm.1, f32[1,2,128,256]{3,2,1,0:T(8,128)} %start_hbm.1, bf16[8,2,128,256]{3,2,1,0:T(8,128)(2,1)} %sens_hbm.1, bf16[1,8,2,128,256]{4,3,2,1,0:T(8,128)(2,1)} %data_hbm.1, ...), custom_call_target="tpu_custom_call" | custom-call | tf_op jit(solution)/shard_map/frame_gradient/pallas_call | solution.py:629
  4.0 0.0 copy-start
  4.0 24.3 %all_to_all.15.mail_ref = f32[8,152,128]{2,1,0:T(8,128)S(1)} all-to-all(f32[8,152,128]{2,1,0:T(8,128)S(1)} %get-tuple-element.13), channel_id=1, replica_groups=mesh['tm'=8,'cuts'=4] {'tm'}, dimensions={0} | all-to-all | bytes 1245184 | tf_op jit(solution)/shard_map/all_to_all | solution.py:617
  28.4 0.0 copy-done
  28.4 3.3 %strip_shrink_gradient.1 = (f32[8,16,128]{2,1,0:T(8,128)S(1)}, f32[32,128]{1,0:T(8,128)S(1)}, f32[8,32,256]{2,1,0:T(8,128)S(1)}, f32[8,32,256]{2,1,0:T(8,128)S(1)}) custom-call(s32[8,128]{1,0:T(8,128)S(1)} %get-tuple-element.12.offsets_ref, f32[8,152,128]{2,1,0:T(8,128)S(1)} %all_to_all.15.mail_ref, f32[8,2,16,256]{3,2,1,0:T(8,128)S(1)} %get-tuple-element.14.sens_ref, ...), custom_call_target="tpu_custom_call" | custom-call | tf_op jit(solution)/shard_map/strip_shrink_gradient/pallas_call | solution.py:662
  31.7 0.0 copy-start.1
  31.7 9.8 %all_to_all.16.heard_ref = f32[8,16,128]{2,1,0:T(8,128)S(1)} all-to-all(f32[8,16,128]{2,1,0:T(8,128)S(1)} %get-tuple-element.16), channel_id=1, replica_groups=mesh['tm'=8,'cuts'=4] {'tm'}, dimensions={0} | all-to-all | bytes 131072 | tf_op jit(solution)/shard_map/all_to_all | solution.py:617
  41.5 0.0 copy-done.1
  41.5 0.9 %strip_shrink.1 = f32[8,32,256]{2,1,0:T(8,128)S(1)} custom-call(s32[8,128]{1,0:T(8,128)S(1)} %get-tuple-element.12.offsets_ref, f32[32,128]{1,0:T(8,128)S(1)} %get-tuple-element.15.own_ref, f32[8,16,128]{2,1,0:T(8,128)S(1)} %all_to_all.16.heard_ref, f32[8,32,256]{2,1,0:T(8,128)S(1)} %get-tuple-element.17.est_ref, ...), custom_call_target="tpu_custom_call" | custom-call | tf_op jit(solution)/shard_map/strip_shrink/pallas_call | solution.py:687
  42.4 10.6 %all_to_all.17.strips_ref = f32[8,32,256]{2,1,0:T(8,128)S(1)} all-to-all(f32[8,32,256]{2,1,0:T(8,128)S(1)} %strip_shrink.1), channel_id=1, replica_groups=mesh['tm'=8,'cuts'=4] {'tm'}, dimensions={0} | all-to-all | bytes 524288 | tf_op jit(solution)/shard_map/all_to_all | solution.py:617
  53.0 0.8 %frame_place.1 = f32[1,2,128,256]{3,2,1,0:T(8,128)} custom-call(s32[8,128]{1,0:T(8,128)S(1)} %get-tuple-element.12.offsets_ref, f32[8,32,256]{2,1,0:T(8,128)S(1)} %all_to_all.17.strips_ref), custom_call_target="tpu_custom_call" | custom-call | tf_op jit(solution)/shard_map/frame_place/pallas_call | solution.py:704
Async XLA Ops:
  4.0 24.3 %copy-start = (bf16[512,512]{1,0:T(8,128)(2,1)S(1)}, bf16[512,512]{1,0:T(8,128)(2,1)}, u32[]{:S(2)}) copy-start(bf16[512,512]{1,0:T(8,128)(2,1)} %constant.4.clone.table_hbm.table_ref) | copy-start | bytes 1572868
  31.7 9.8 %copy-start.1 = (f32[64,128]{1,0:T(8,128)S(1)}, f32[64,128]{1,0:T(8,128)}, u32[]{:S(2)}) copy-start(f32[64,128]{1,0:T(8,128)} %constant.5.clone.select_ref) | copy-start | bytes 98308
